TPU v7x, 32 devices: a whole 2x2x4 slice. The times are simulated.
32 devices in a mesh: member: 4 (over z), tile: 8 (over y, x, core).
Axes of the slice: x: 2, y: 2, z: 4, core: 2. Of those that a mesh axis runs over, the one named last changes fastest.
Arguments:
- teacher_logits: bfloat16 [16, 1024, 4096], P('member', 'tile'), may hold values from -8 to 260
- coverage: int32 [1024], P('tile'), may hold values from 0 to 7, as said below
- features: bfloat16 [4, 256, 64, 256], P('member', 'tile'), may hold values from -6 to 6
- labels: int32 [4, 256, 64], P('member', 'tile'), may hold values from 0 to 63
- first_weight: bfloat16 [3, 3, 256, 256], replicated, may hold values from -0.125 to 0.125
- second_weight: bfloat16 [3, 3, 256, 256], replicated, may hold values from -0.125 to 0.125
- head_weight: bfloat16 [256, 64], replicated, may hold values from -0.375 to 0.375
Outputs:
- first_kernel_grad: float32 [3, 3, 256, 256], replicated
- second_kernel_grad: float32 [3, 3, 256, 256], replicated
- head_kernel_grad: float32 [256, 64], replicated
- loss_value: float32 [], replicated
Inputs may be any that keep to these rules, and one draw needn't show every extreme that they name: Slot k of column t goes to column coverage[t * 128 + k]; for every slot each column receives it from exactly one column. Within each block of 32 consecutive slots a column sends at most 8 tiles to any one column and exactly 8 to one; over all 128 slots at most 32 to any one column, reached.
All inputs are finite; a program needn't handle non-finite values.
Results may differ from a plain program's by a relative error of at most 0.013.
The roundings to bfloat16 on the way count: a program that leaves them out, or rounds other values in their place, can miss the bound.
Values may be sent and summed in bfloat16 or wider, within the bound.
No kernel may reach another device: no remote copies, remote signals or barrier semaphores. Data moves between devices by JAX's collectives and lax.ppermute only.
A program may use at most 128 MiB of HBM per device.

v0:
```python
import functools
import math

import jax
import jax.numpy as jnp
from jax import lax
from jax.experimental import pallas as pl
from jax.experimental.pallas import tpu as pltpu
from jax.sharding import PartitionSpec as P

BF16 = jnp.bfloat16
F32 = jnp.float32
LANES = 128
MXU = 256


def whole(count):
    return [pl.BlockSpec(memory_space=pltpu.VMEM)] * count


def iota(shape, axis):
    return lax.broadcasted_iota(jnp.int32, shape, axis)


def dot(left, right):
    return jnp.dot(left, right, preferred_element_type=F32)


def split_lanes(value):
    high = value.astype(BF16).astype(F32)
    return jnp.where(iota(value.shape, 1) < 64, high, value - high).astype(BF16)


def join_lanes(value):
    return value + pltpu.roll(value, 64, 1)


def class_sums(value, classes):
    pick = (iota((MXU, LANES), 0) // classes == iota((MXU, LANES), 1) % (MXU // classes)).astype(BF16)
    high = value.astype(BF16)
    low = (value - high.astype(F32)).astype(BF16)
    return dot(high, pick) + dot(low, pick)


def hbm(count):
    return [pl.BlockSpec(memory_space=pl.ANY)] * count


def scalars():
    return pl.BlockSpec(memory_space=pltpu.SMEM)


CORE, CHIP, MEMBER, DEVICE, FIRST, LAST = range(6)


def teacher_kernel(classes, flip, logit_hbm, *refs):
    member = lax.axis_index("member")
    near_ref, own_ref, x_ref, sum_ref, acc_ref, sems = refs[-6:]
    quarters, members, tiles, width = x_ref.shape
    parts = width // MXU
    per = MXU // classes
    tile_rows = pl.ds(pl.multiple_of(((member // 2) ^ flip) * tiles, tiles), tiles)
    arrive = [
        pltpu.make_async_copy(logit_hbm.at[:, tile_rows, pl.ds(i * width, width)], x_ref.at[i], sems.at[i])
        for i in range(quarters)
    ]
    for copy in arrive:
        copy.start()
    same = (iota((MXU, MXU), 0) // classes == iota((MXU, MXU), 1) // classes).astype(BF16)
    acc_ref[...] = jnp.zeros_like(acc_ref)

    @pl.loop(0, quarters)
    def _(i):
        pltpu.make_async_copy(logit_hbm.at[:, tile_rows, pl.ds(0, width)], x_ref.at[i], sems.at[i]).wait()
        each = range(parts)
        x = [x_ref[i, :, :, n * MXU : (n + 1) * MXU].astype(F32).reshape(members * tiles, MXU) for n in each]
        root = [jnp.exp(one * 0.25) for one in x]
        total = [dot(one.astype(BF16), same) for one in root]
        root = [one * pl.reciprocal(whole_sum, approx=True) for one, whole_sum in zip(root, total)]
        square = [one * one for one in root]
        power = [one * one for one in square]
        total = [dot(one.astype(BF16), same) for one in power]
        inverse = [pl.reciprocal(one, approx=True) for one in total]
        inverse = [one * (2.0 - whole_sum * one) for one, whole_sum in zip(inverse, total)]
        probs = [(one * other).reshape(members, tiles, MXU) for one, other in zip(power, inverse)]
        first = [functools.reduce(jnp.add, [one[m] for m in range(members)]) for one in probs]
        within = [
            functools.reduce(jnp.add, [one[m] * one[m] for m in range(members)]) - sums * sums * (1.0 / members)
            for one, sums in zip(probs, first)
        ]
        sums = [class_sums(one, classes) for one in within]
        acc = acc_ref[...]
        for n in each:
            acc = jnp.where(iota(acc.shape, 1) % 64 // per == i * parts + n, sums[n], acc)
        acc_ref[...] = acc
        for n in each:
            sum_ref[:, pl.ds(pl.multiple_of(i * width + n * MXU, MXU), MXU)] = first[n].astype(BF16)

    sum_ref[:, quarters * width :] = split_lanes(acc_ref[...])
    block = tiles // 2
    odd = 1 - member % 2
    near_ref[...] = sum_ref[pl.ds(pl.multiple_of(odd * block, 16), block), :]
    own_ref[...] = sum_ref[pl.ds(pl.multiple_of((1 - odd) * block, 16), block), :]


def teacher_moments(logits, tiles, classes, flip, *earlier):
    members, _, width = logits.shape
    quarters = 4
    shape = jax.ShapeDtypeStruct
    outs = [shape((tiles, width + LANES), BF16)] * 2
    return pl.pallas_call(
        functools.partial(teacher_kernel, classes, flip),
        in_specs=hbm(1 + len(earlier)),
        out_specs=whole(len(outs)),
        out_shape=outs,
        scratch_shapes=[
            pltpu.VMEM((quarters, members, 2 * tiles, width // quarters), BF16),
            pltpu.VMEM((2 * tiles, width + LANES), BF16),
            pltpu.VMEM((2 * tiles, LANES), F32),
            pltpu.SemaphoreType.DMA((quarters,)),
        ],
        compiler_params=pltpu.CompilerParams(vmem_limit_bytes=58 << 20),
        cost_estimate=pl.CostEstimate(flops=1_500_000_000, bytes_accessed=2_600_000, transcendentals=3_000_000),
        name="teacher_moments",
    )(logits, *earlier)


def combine_kernel(classes, members, columns, capacity, where_ref, cover_ref, after_ref, *refs):
    chips = columns // 2
    got_refs, out_refs = refs[:-chips], refs[-chips:]
    groups = len(got_refs)
    tiles, extended = got_refs[0].shape
    width = extended - LANES
    means, gaps = [], []
    for start in range(0, width, MXU):
        sums = [got_ref[:, start : start + MXU].astype(F32) for got_ref in got_refs]
        total = sums[0]
        for one in sums[1:]:
            total = total + one
        mean = total * (1.0 / (members * groups))
        means.append(mean.astype(BF16))
        gap = jnp.zeros_like(mean)
        for one in sums:
            off = one * (1.0 / members) - mean
            gap = gap + off * off
        gaps.append(gap)
    between = class_sums(jnp.concatenate(gaps, axis=0), classes)
    lane = iota((tiles, LANES), 1)
    spread = jnp.zeros((tiles, LANES), F32)
    per = MXU // classes
    for i in range(width // MXU):
        spread = jnp.where(lane % 64 // per == i, between[i * tiles : (i + 1) * tiles], spread)
    inner = got_refs[0][:, width:].astype(F32)
    for got_ref in got_refs[1:]:
        inner = inner + got_ref[:, width:].astype(F32)
    spread = spread * (1.0 / groups) + join_lanes(inner) * (1.0 / (members * groups))
    index = (iota((tiles, LANES), 0) + 1).astype(F32).astype(BF16)
    rows = jnp.concatenate([*means, split_lanes(spread), index], axis=1)
    target = cover_ref[where_ref[MEMBER]] ^ (where_ref[CHIP] * 2 + where_ref[CORE])
    onehot = (iota((columns, tiles), 0) == target).astype(F32)
    earlier = (iota((tiles, tiles), 0) < iota((tiles, tiles), 1)).astype(BF16)
    before = dot(onehot.astype(BF16), earlier)
    rank = jnp.sum(before * onehot, axis=0, keepdims=True).astype(jnp.int32)
    place = (iota((columns * capacity, tiles), 0) == target * capacity + rank).astype(BF16)
    sent = dot(place, rows)
    for index, out_ref in enumerate(out_refs):
        out_ref[...] = sent[2 * index * capacity : 2 * (index + 1) * capacity].astype(BF16)


def combine(got, cover, where, after, classes, members, columns, capacity):
    extended = got[0].shape[1]
    return pl.pallas_call(
        functools.partial(combine_kernel, classes, members, columns, capacity),
        in_specs=[pl.BlockSpec(memory_space=pltpu.SMEM), *whole(1), pl.BlockSpec(memory_space=pl.ANY), *whole(len(got))],
        out_specs=whole(columns // 2),
        out_shape=[jax.ShapeDtypeStruct((2 * capacity, extended + LANES), BF16)] * (columns // 2),
        compiler_params=pltpu.CompilerParams(vmem_limit_bytes=12 << 20),
        cost_estimate=pl.CostEstimate(flops=100_000_000, bytes_accessed=1_700_000, transcendentals=0),
        name="combine",
    )(where, cover, after, *got)


def put_shifted(ref, start, value, shift, width):
    rows, channels = value.shape
    col = iota(value.shape, 0) % width
    left = jnp.where(col >= shift, pltpu.roll(value, shift, 0), 0.0)
    right = jnp.where(col < width - shift, pltpu.roll(value, rows - shift, 0), 0.0)
    ref[pl.ds(start, rows), :channels] = left.astype(BF16)
    ref[pl.ds(start, rows), channels : 2 * channels] = value.astype(BF16)
    ref[pl.ds(start, rows), 2 * channels :] = right.astype(BF16)


def three_dots(ref, start, step, rows, weight_ref):
    total = None
    for tap in range(3):
        part = dot(ref[pl.ds(start + tap * step, rows), :], weight_ref[tap])
        total = part if total is None else total + part
    return total


def turned_dot(left, right):
    return lax.dot_general(left, right, (((1,), (1,)), ((), ())), preferred_element_type=F32)


def turned_dot(left, right):
    return lax.dot_general(left, right, (((1,), (1,)), ((), ())), preferred_element_type=F32)


def student_kernel(
    width, place_ref, before_ref, after_ref, head_ref, label_ref, x_ref, first_ref, second_ref, own_ref,
    one_ref, two_ref, log_ref, base_ref, label_sum_ref, xcat, hcat, logit_ref,
):
    cells, channels = x_ref.shape
    halo = before_ref.shape[0]
    block = 4 * width
    put_shifted(xcat, 0, before_ref[...].astype(F32), 1, width)
    put_shifted(xcat, halo + cells, after_ref[...].astype(F32), 1, width)
    for start in range(0, cells, block):
        put_shifted(xcat, halo + start, x_ref[start : start + block, :].astype(F32), 1, width)
    lines = cells // width
    low = jnp.where(place_ref[FIRST] == 1, 2, 0)
    high = jnp.where(place_ref[LAST] == 1, lines + 2, lines + 4)
    for start in range(0, cells + block, block):
        value = jnp.maximum(three_dots(xcat, start, width, block, first_ref), 0.0)
        if start == 0 or start == cells:
            line = start // width + iota(value.shape, 0) // width
            value = jnp.where((line >= low) & (line < high), value, 0.0)
        put_shifted(hcat, start, value, 2, width)
        one_ref[start : start + block, :] = value.astype(BF16)
    head = jnp.concatenate([head_ref[...], head_ref[...]], axis=0)
    for start in range(0, cells, block):
        rows = slice(start, start + block)
        two = jnp.maximum(three_dots(hcat, start, 2 * width, block, second_ref), 0.0).astype(BF16)
        two_ref[rows, :] = two
        logit_ref[rows, :] = turned_dot(two, head)

    tiles, pixels = label_ref.shape
    edge = math.isqrt(pixels)
    across = width // edge
    lane = iota((tiles, LANES), 1)
    even = lane < 64
    label_sum = jnp.zeros((tiles, LANES), F32)
    for pair in range(pixels // 2):
        row, col = 2 * pair // edge, 2 * pair % edge
        parts = []
        for down in range(tiles // across):
            start = (down * edge + row) * width + col
            left = logit_ref[pl.ds(start, across, stride=edge), :]
            right = logit_ref[pl.ds(start + 1, across, stride=edge), :]
            parts.append(jnp.where(iota(left.shape, 1) < 64, left, right))
        value = jnp.concatenate(parts, axis=0)
        top = jnp.where(
            even,
            jnp.max(jnp.where(even, value, -jnp.inf), axis=1, keepdims=True),
            jnp.max(jnp.where(even, -jnp.inf, value), axis=1, keepdims=True),
        )
        value = value - top
        power = jnp.exp(value)
        total = jnp.where(
            even,
            jnp.sum(jnp.where(even, power, 0.0), axis=1, keepdims=True),
            jnp.sum(jnp.where(even, 0.0, power), axis=1, keepdims=True),
        )
        value = value - jnp.log(total)
        label = jnp.where(even, label_ref[:, 2 * pair : 2 * pair + 1], label_ref[:, 2 * pair + 1 : 2 * pair + 2])
        hit = label == lane % 64
        label_sum = label_sum + jnp.where(hit, value, 0.0)
        log_ref[pair * tiles : (pair + 1) * tiles, :] = value
        base_ref[pair * tiles : (pair + 1) * tiles, :] = jnp.exp(value) - hit.astype(F32)
    label_sum_ref[...] = label_sum


def student_forward(place, before, after, head, labels, x, first, second, own, width):
    cells, channels = x.shape
    halo = before.shape[0]
    tiles, pixels = labels.shape
    shape = jax.ShapeDtypeStruct
    return pl.pallas_call(
        functools.partial(student_kernel, width),
        in_specs=[scalars(), *whole(7), *hbm(1)],
        out_specs=whole(5),
        out_shape=[
            shape((cells + 4 * width, channels), BF16),
            shape((cells, channels), BF16),
            shape((cells // 2, LANES), F32),
            shape((cells // 2, LANES), F32),
            shape((tiles, LANES), F32),
        ],
        scratch_shapes=[
            pltpu.VMEM((cells + 2 * halo, 3 * channels), BF16),
            pltpu.VMEM((cells + 4 * width, 3 * channels), BF16),
            pltpu.VMEM((cells, LANES), F32),
        ],
        compiler_params=pltpu.CompilerParams(vmem_limit_bytes=24 << 20),
        cost_estimate=pl.CostEstimate(flops=6_000_000_000, bytes_accessed=12_000_000, transcendentals=500_000),
        name="student_forward",
    )(place, before, after, head, labels, x, first, second, own)


def put_turned(ref, start, value, shift, width):
    rows, channels = value.shape
    col = iota(value.shape, 0) % width
    left = jnp.where(col >= shift, pltpu.roll(value, shift, 0), 0.0)
    right = jnp.where(col < width - shift, pltpu.roll(value, rows - shift, 0), 0.0)
    for tap, one in enumerate((left, value, right)):
        ref[tap * channels : (tap + 1) * channels, pl.ds(start, rows)] = one.T.astype(BF16)


def turn_kernel(
    width, before_ref, x_ref, after_ref, one_ref, two_ref, second_ref, xt_ref, ht_ref, twot_ref, wt_ref
):
    cells, channels = x_ref.shape
    halo = before_ref.shape[0]
    pair = 2 * width
    first = jnp.concatenate([before_ref[halo - width :], x_ref[:width]], axis=0).astype(F32)
    put_turned(xt_ref, 0, first, 1, width)
    last = jnp.concatenate([x_ref[cells - width :], after_ref[:width]], axis=0).astype(F32)
    put_turned(xt_ref, cells, last, 1, width)

    for start in range(pair, cells, pair):
        put_turned(xt_ref, start, x_ref[start - width : start + width, :].astype(F32), 1, width)
    for start in range(0, one_ref.shape[0], pair):
        put_turned(ht_ref, start, one_ref[start : start + pair, :].astype(F32), 2, width)
    for start in range(0, cells, MXU):
        twot_ref[:, start : start + MXU] = two_ref[start : start + MXU, :].astype(F32).T.astype(BF16)
    for i in range(3):
        for tap in range(3):
            part = slice(tap * channels, (tap + 1) * channels)
            mirror = slice((2 - tap) * channels, (3 - tap) * channels)
            wt_ref[i, part, :] = second_ref[i, mirror, :].astype(F32).T.astype(BF16)


def turn(before, x, after, one, two, second, width):
    cells, channels = x.shape
    shape = jax.ShapeDtypeStruct
    return pl.pallas_call(
        functools.partial(turn_kernel, width),
        in_specs=whole(6),
        out_specs=whole(4),
        out_shape=[
            shape((3 * channels, cells + 2 * width), BF16),
            shape((3 * channels, cells + 4 * width), BF16),
            shape((channels, cells), BF16),
            shape((3, 3 * channels, channels), BF16),
        ],
        compiler_params=pltpu.CompilerParams(vmem_limit_bytes=20 << 20),
        cost_estimate=pl.CostEstimate(flops=3_000_000_000, bytes_accessed=14_000_000, transcendentals=0),
        name="turn",
    )(before, x, after, one, two, second)


def head_kernel(
    scale, width, log_ref, base_ref, label_sum_ref, two_ref, twot_ref, head_ref, *refs
):
    *got_refs, grad_ref, top_ref, bottom_ref, head_grad_ref, got_ref, natural = refs
    slots, extended = got_ref.shape
    held = [one[...].astype(F32) for one in got_refs]
    held = [one[: one.shape[0] // 2] for one in held[:-1]] + held[-1:]
    got_ref[...] = jnp.concatenate(held, axis=0).astype(BF16)
    tiles = label_sum_ref.shape[0]
    flat = extended - 2 * LANES
    pixels = flat // 64
    edge = math.isqrt(pixels)
    across = width // edge
    index = got_ref[:, flat + LANES :].astype(F32)
    take = (index == (iota((slots, LANES), 1) + 1).astype(F32)).astype(F32).T[:tiles].astype(BF16)
    spread = join_lanes(dot(take, got_ref[:, flat : flat + LANES]))
    weight = 1.0 / (0.1 + spread)
    even = iota((tiles, LANES), 1) < 64
    loss = -label_sum_ref[...]
    for pair in range(pixels // 2):
        rows = slice(pair * tiles, (pair + 1) * tiles)
        if pair % 2 == 0:
            both = dot(take, got_ref[:, pair * LANES : (pair + 2) * LANES])
        mean = both[:, pair % 2 * LANES : (pair % 2 + 1) * LANES]
        cell = jnp.where(even, weight[:, 2 * pair : 2 * pair + 1], weight[:, 2 * pair + 1 : 2 * pair + 2])
        value = log_ref[rows, :]
        held = mean > 0
        loss = loss + cell * jnp.where(held, mean * (jnp.log(jnp.where(held, mean, 1.0)) - value), 0.0)
        grad = (cell * (jnp.exp(value) - mean) + base_ref[rows, :]) * scale
        turned = pltpu.roll(grad, 64, 1)
        row, col = 2 * pair // edge, 2 * pair % edge
        for down in range(tiles // across):
            start = (down * edge + row) * width + col
            natural[pl.ds(start, across, stride=edge), :] = grad[down * across : (down + 1) * across]
            natural[pl.ds(start + 1, across, stride=edge), :] = turned[down * across : (down + 1) * across]
    cells, channels = two_ref.shape
    logit_grad = natural[...].astype(BF16)
    head = jnp.concatenate([head_ref[...], jnp.zeros_like(head_ref)], axis=0)
    head_grad_ref[:channels, :] = dot(twot_ref[...], logit_grad)
    head_grad_ref[channels:, :] = loss
    block = 4 * width
    for start in range(0, cells, block):
        rows = slice(start, start + block)
        grad = dot(logit_grad[rows], head)
        grad_ref[rows, :] = jnp.where(two_ref[rows, :].astype(F32) > 0, grad, 0.0).astype(BF16)
    top_ref[...] = grad_ref[: 2 * width, :]
    bottom_ref[...] = grad_ref[cells - 2 * width :, :]


def head_step(got, log, base, label_sum, two, twot, head, scale, width):
    cells, channels = two.shape
    shape = jax.ShapeDtypeStruct
    return pl.pallas_call(
        functools.partial(head_kernel, scale, width),
        in_specs=whole(6 + len(got)),
        out_specs=whole(4),
        out_shape=[
            shape((cells, channels), BF16),
            shape((2 * width, channels), BF16),
            shape((2 * width, channels), BF16),
            shape((channels + label_sum.shape[0], LANES), F32),
        ],
        scratch_shapes=[
            pltpu.VMEM((2 * got[-1].shape[0], got[-1].shape[1]), BF16),
            pltpu.VMEM((cells, LANES), F32),
        ],
        compiler_params=pltpu.CompilerParams(vmem_limit_bytes=14 << 20),
        cost_estimate=pl.CostEstimate(flops=400_000_000, bytes_accessed=5_000_000, transcendentals=500_000),
        name="head_step",
    )(log, base, label_sum, two, twot, head, *got)


def inner_dots(ref, start, step, rows, weight_ref):
    total = None
    for tap in range(3):
        part = dot(ref[start + (2 - tap) * step : start + (2 - tap) * step + rows, :], weight_ref[tap])
        total = part if total is None else total + part
    return total


def second_kernel(width, ht_ref, grad_ref, wt_ref, one_ref, out_ref, inner_ref, gcat):
    cells, channels = grad_ref.shape
    block = 4 * width
    halo = 2 * width
    for start in range(0, cells, block):
        put_shifted(gcat, start, grad_ref[start : start + block, :].astype(F32), 2, width)
    for tap in range(3):
        part = dot(ht_ref[:, halo * tap : halo * tap + cells], grad_ref[...])
        out_ref[tap * 3 * channels : (tap + 1) * 3 * channels, :] = part.astype(BF16)
    for start in range(block, cells - block, block):
        value = inner_dots(gcat, start - halo, halo, block, wt_ref)
        held = one_ref[halo + start : halo + start + block, :].astype(F32) > 0
        inner_ref[start - block : start, :] = jnp.where(held, value, 0.0).astype(BF16)


def second_step(ht, grad, wt, one, width):
    cells, channels = grad.shape
    return pl.pallas_call(
        functools.partial(second_kernel, width),
        in_specs=whole(4),
        out_specs=whole(2),
        out_shape=[
            jax.ShapeDtypeStruct((9 * channels, channels), BF16),
            jax.ShapeDtypeStruct((cells - 8 * width, channels), BF16),
        ],
        scratch_shapes=[pltpu.VMEM((cells, 3 * channels), BF16)],
        compiler_params=pltpu.CompilerParams(vmem_limit_bytes=20 << 20),
        cost_estimate=pl.CostEstimate(flops=4_500_000_000, bytes_accessed=9_000_000, transcendentals=0),
        name="second_step",
    )(ht, grad, wt, one)


def first_kernel(width, plan, place_ref, before_ref, after_ref, grad_ref, head_grad_ref, second_ref, inner_ref, *refs):
    wt_ref, one_ref, xt_ref, *refs = refs
    chips, groups, near_rows, far_rows = plan
    keep_refs, give_refs, refs = refs[: chips + 1], refs[chips + 1 : 2 * chips + 2], refs[2 * chips + 2 :]
    gtop, gbottom, padded, halves, sem = refs
    cells, channels = grad_ref.shape
    rows = 9 * channels
    used = rows + channels // 2
    half = halves.shape[1]
    second_copy = pltpu.make_async_copy(second_ref, halves.at[1, pl.ds(0, rows)], sem)
    second_copy.start()
    halo = before_ref.shape[0]
    block = 4 * width
    inside = 3 * halo
    put_shifted(gtop, 0, before_ref[...].astype(F32), 2, width)
    put_shifted(gtop, halo, grad_ref[:inside, :].astype(F32), 2, width)
    put_shifted(gbottom, 0, grad_ref[cells - inside :, :].astype(F32), 2, width)
    put_shifted(gbottom, inside, after_ref[...].astype(F32), 2, width)
    padded[:halo, :] = jnp.zeros((halo, channels), BF16)
    padded[halo + cells :, :] = jnp.zeros((halo, channels), BF16)
    padded[halo + block : halo + cells - block, :] = inner_ref[...]
    for ref, start in ((gtop, 0), (gbottom, cells - block)):
        value = inner_dots(ref, 0, halo, block, wt_ref)
        held = one_ref[halo + start : halo + start + block, :].astype(F32) > 0
        padded[halo + start : halo + start + block, :] = jnp.where(held, value, 0.0).astype(BF16)
    span = cells + 2 * width
    for tap in range(3):
        part = dot(xt_ref[...], padded[(2 - tap) * width : (2 - tap) * width + span, :])
        halves[0, tap * 3 * channels : (tap + 1) * 3 * channels, :] = part.astype(BF16)
    lane = iota((channels // 2, LANES), 1)
    loss = jnp.sum(head_grad_ref[channels:, :])
    high = loss.astype(BF16).astype(F32)
    extra = jnp.where(lane == 64, high, jnp.where(lane == 65, loss - high, 0.0))
    extra = jnp.where(iota(lane.shape, 0) == place_ref[DEVICE] % (channels // 2), extra, 0.0)
    for side in range(2):
        value = jnp.where(lane < 64, head_grad_ref[side * channels // 2 : (side + 1) * channels // 2, :], extra)
        halves[0, rows:used, side * LANES : (side + 1) * LANES] = value.astype(BF16)
    if half > used:
        halves[0, used:, :] = jnp.zeros((half - used, channels), BF16)
    halves[1, rows:, :] = jnp.zeros((half - rows, channels), BF16)
    second_copy.wait()
    core, chip = place_ref[CORE], place_ref[CHIP]
    size = groups * near_rows
    for step in range(chips):
        low = pl.multiple_of((chip ^ step) * size, 16)
        give_refs[step][...] = halves[1 - core, pl.ds(low, size), :]
        keep_refs[step][...] = halves[core, pl.ds(low, size), :]
    give_refs[chips][...] = halves[1 - core, chips * size :, :]
    keep_refs[chips][...] = halves[core, chips * size :, :]


def first_step(place, before, after, grad, head_grad, second, inner, wt, one, xt, width, plan):
    cells, channels = grad.shape
    halo = before.shape[0]
    chips, groups, near_rows, far_rows = plan
    half_rows = chips * groups * (near_rows + far_rows)
    piece = [jax.ShapeDtypeStruct((groups * near_rows, channels), BF16)] * chips
    piece += [jax.ShapeDtypeStruct((chips * groups * far_rows, channels), BF16)]
    outs = pl.pallas_call(
        functools.partial(first_kernel, width, plan),
        in_specs=[scalars(), *whole(9)],
        out_specs=whole(2 * chips + 2),
        out_shape=piece * 2,
        scratch_shapes=[
            pltpu.VMEM((4 * halo, 3 * channels), BF16),
            pltpu.VMEM((4 * halo, 3 * channels), BF16),
            pltpu.VMEM((cells + 4 * width, channels), BF16),
            pltpu.VMEM((2, half_rows, channels), BF16),
            pltpu.SemaphoreType.DMA,
        ],
        compiler_params=pltpu.CompilerParams(vmem_limit_bytes=24 << 20),
        cost_estimate=pl.CostEstimate(flops=5_000_000_000, bytes_accessed=10_000_000, transcendentals=0),
        name="first_step",
    )(place, before, after, grad, head_grad, second, inner, wt, one, xt)
    return (outs[: chips + 1], outs[chips + 1 :])


def neighbours(first, last, axis):
    count = lax.axis_size(axis)
    up = [(i, i + 1) for i in range(count - 1)]
    down = [(i + 1, i) for i in range(count - 1)]
    return (lax.ppermute(last, axis, up), lax.ppermute(first, axis, down))


def pairwise(array, axis, step):
    count = lax.axis_size(axis)
    return lax.ppermute(array, axis, [(i, i ^ step) for i in range(count)])


def add(arrays):
    return functools.reduce(jnp.add, [array.astype(F32) for array in arrays]).astype(BF16)


def assemble_kernel(width, plan, cell_total, place_ref, *refs):
    chips, groups, near_rows, far_rows = plan
    pieces, refs = refs[: chips + 1], refs[chips + 1 :]
    own = len(refs) == 5
    if own:
        first_ref, second_ref, extra_ref, value_ref, sem = refs
    else:
        _, _, held_ref, first_ref, second_ref, head_ref, loss_ref, value_ref, sem = refs
    grad_rows = first_ref.shape[0]
    core, chip, member = place_ref[CORE], place_ref[CHIP], place_ref[MEMBER]
    for s in range(chips):
        value = pieces[s][...].astype(F32)
        for u in range(groups):
            start = pl.multiple_of(((chip ^ s) * groups + (member ^ u)) * near_rows, 8)
            value_ref[pl.ds(start, near_rows), :] = value[u * near_rows : (u + 1) * near_rows]
    value = pieces[chips][...].astype(F32)
    for u in range(groups):
        for s in range(chips):
            low = (u * chips + s) * far_rows
            start = chips * groups * near_rows + ((member ^ u) * chips + (chip ^ s)) * far_rows
            value_ref[pl.ds(pl.multiple_of(start, 8), far_rows), :] = value[low : low + far_rows]
    half = core if own else 1 - core
    filled = value_ref.at[pl.ds(0, grad_rows)]

    @pl.when(half == 0)
    def _():
        pltpu.make_async_copy(filled, first_ref, sem).start()

    @pl.when(half != 0)
    def _():
        pltpu.make_async_copy(filled, second_ref, sem).start()

    rows = width // 2
    extra = value_ref[grad_rows : grad_rows + rows, :]
    if own:
        extra_ref[...] = extra
    else:
        extra = jnp.where(core == 0, held_ref[...], extra)
        for side in range(2):
            part = extra[:, side * LANES : (side + 1) * LANES].T
            head_ref[:, side * rows : (side + 1) * rows] = part[: head_ref.shape[0]]
        lane = iota(extra.shape, 1)
        loss = jnp.sum(jnp.where((lane == 64) | (lane == 65), extra, 0.0), keepdims=True)
        loss_ref[...] = loss / cell_total
    pltpu.make_async_copy(filled, first_ref, sem).wait()


def assemble(place, pieces, plan, grad_rows, classes, cell_total):
    chips, groups, near_rows, far_rows = plan
    half_rows = chips * groups * (near_rows + far_rows)
    width = pieces[0].shape[1]
    shape = jax.ShapeDtypeStruct
    totals = [shape((grad_rows, width), F32)] * 2
    extra = shape((width // 2, width), F32)
    common = dict(
        scratch_shapes=[pltpu.VMEM((half_rows, width), F32), pltpu.SemaphoreType.DMA],
        compiler_params=pltpu.CompilerParams(vmem_limit_bytes=48 << 20),
        cost_estimate=pl.CostEstimate(flops=1_000_000, bytes_accessed=3_700_000, transcendentals=0),
        name="assemble",
    )
    kernel = functools.partial(assemble_kernel, width, plan, cell_total)
    count = chips + 1
    held = pl.pallas_call(
        kernel,
        in_specs=[scalars(), *whole(count)],
        out_specs=[*hbm(2), *whole(1)],
        out_shape=[*totals, extra],
        **common,
    )(place, *pieces[:count])
    return pl.pallas_call(
        kernel,
        in_specs=[scalars(), *whole(count), *hbm(2), *whole(1)],
        out_specs=[*hbm(2), *whole(2)],
        out_shape=[*totals, shape((classes, width), F32), shape((1, 1), F32)],
        input_output_aliases={count + 1: 0, count + 2: 1},
        **common,
    )(place, *pieces[count:], *held)


def gradient_pieces(place, keep, give, plan):
    chips, groups, near_rows, far_rows = plan
    got = [pairwise(one, "core", 1) for one in give]
    near = [add(pair) for pair in zip(keep[:chips], got[:chips])]
    far = [keep[chips], got[chips]]

    def block(arrays, axis, me, step, rows):
        start = (me ^ step) * rows
        return add([lax.dynamic_slice_in_dim(one, start, rows, axis=0) for one in arrays])

    chip, member = place[CHIP], place[MEMBER]
    far = [block(far, "member", member, step, chips * far_rows) for step in range(groups)]
    near = [near[0]] + [pairwise(near[step], "chip", step) for step in range(1, chips)]
    far = [far[0]] + [pairwise(far[step], "member", step) for step in range(1, groups)]
    near = [block(near, "member", member, step, near_rows) for step in range(groups)]
    far = [block(far, "chip", chip, step, far_rows) for step in range(chips)]
    near = add([near[0]] + [pairwise(near[step], "member", step) for step in range(1, groups)])
    far = add([far[0]] + [pairwise(far[step], "chip", step) for step in range(1, chips)])

    near = jnp.concatenate([near] + [pairwise(near, "member", step) for step in range(1, groups)], axis=0)
    far = jnp.concatenate([far] + [pairwise(far, "chip", step) for step in range(1, chips)], axis=0)
    near, far = lax.optimization_barrier((near, far))
    held = [near] + [pairwise(near, "chip", step) for step in range(1, chips)]
    far = jnp.concatenate([far] + [pairwise(far, "member", step) for step in range(1, groups)], axis=0)
    held += [far]
    return held + [pairwise(piece, "core", 1) for piece in held]


def body(teacher_logits, coverage, features, labels, first_weight, second_weight, head_weight):
    channels, classes = head_weight.shape
    members, tiles_here, flat_width = teacher_logits.shape
    pixels = flat_width // classes
    edge = math.isqrt(pixels)
    groups = lax.axis_size("member")
    chips = lax.axis_size("chip")
    columns = chips * 2
    tile_axes = ("chip", "core")
    block_tiles = tiles_here // groups
    capacity = max(2, 2 * block_tiles // columns)
    local = features[0]
    lines, width = local.shape[:2]
    cells = lines * width
    cell_total = groups * columns * cells
    column = lax.axis_index(tile_axes)
    place = jnp.stack(
        [
            lax.axis_index("core"),
            lax.axis_index("chip"),
            lax.axis_index("member"),
            lax.axis_index(("member", *tile_axes)),
            column == 0,
            column == columns - 1,
        ]
    ).astype(jnp.int32)
    flat = local.reshape(cells, channels)
    first_rows = first_weight.reshape(3, 3 * channels, channels)
    second_rows = second_weight.reshape(3, 3 * channels, channels)
    head = head_weight.T

    before, after = neighbours(flat[: 3 * width], flat[cells - 3 * width :], tile_axes)
    far = teacher_moments(teacher_logits, block_tiles, classes, 1)
    got = [pairwise(one, "member", step) for step, one in zip((3, 2), far)]
    near, own = teacher_moments(teacher_logits, block_tiles, classes, 0)
    got += [pairwise(near, "member", 1), own]
    label_rows = (
        labels[0].reshape(lines // edge, edge, width // edge, edge).transpose(0, 2, 1, 3).reshape(block_tiles, pixels)
    )
    one, two, log, base, label_sum = student_forward(
        place, before, after, head, label_rows, flat, first_rows, second_rows, own, width
    )
    xt, ht, twot, wt = turn(before, flat, after, one, two, second_rows, width)
    cover = coverage.reshape(groups, 1, block_tiles)
    sent = combine(got, cover, place, twot, classes, members, columns, capacity)
    received = [sent[0]] + [pairwise(sent[step], "chip", step) for step in range(1, chips)]
    passed = pairwise(jnp.concatenate([piece[capacity:] for piece in received], axis=0), "core", 1)
    received = [*received, passed]
    grad_two, top, bottom, head_grad = head_step(
        received, log, base, label_sum, two, twot, head, 1.0 / math.sqrt(cell_total), width
    )
    grad_before, grad_after = neighbours(top, bottom, tile_axes)
    second, inner = second_step(ht, grad_two, wt, one, width)
    rows, extra_rows = 9 * channels, channels // 2
    unit = 8 * groups * chips
    block_rows = -(-(rows + extra_rows) // unit) * 8
    far_rows = block_rows // 24 * 8
    plan = (chips, groups, block_rows - far_rows, far_rows)
    keep, give = first_step(
        place, grad_before, grad_after, grad_two, head_grad, second, inner, wt, one, xt, width, plan
    )
    pieces = gradient_pieces(place, keep, give, plan)
    first_total, second_total, head_total, loss = assemble(
        place, pieces, plan, rows, classes, cell_total
    )
    kernel_shape = (3, 3, channels, channels)
    return (first_total.reshape(kernel_shape), second_total.reshape(kernel_shape), head_total.T, loss[0, 0])


def solution(mesh):
    groups, columns = mesh.shape["member"], mesh.shape["tile"]
    split = jax.sharding.Mesh(mesh.devices.reshape(groups, columns // 2, 2), ("member", "chip", "core"))
    tile = ("chip", "core")
    return jax.shard_map(
        body,
        mesh=split,
        in_specs=(
            P("member", tile, None),
            P(tile),
            P("member", tile, None, None),
            P("member", tile, None),
            P(),
            P(),
            P(),
        ),
        out_specs=(P(), P(), P(), P()),
        check_vma=False,
    )
```

profile of v0, /device:TPU:1, one launch (start us, length us, event | category | flops | bytes accessed | tf_op | source)
XLA Modules:
  0.0 124.2 jit_solution(7376430928838758057)
XLA Ops:
  0.6 1.6 %fusion = (bf16[1,3,64,256]{3,2,1,0:T(8,128)(2,1)}, bf16[1,3,64,256]{3,2,1,0:T(8,128)(2,1)}) fusion(bf16[1,32,64,256]{3,2,1,0:T(8,128)(2,1)} %param.9), kind=kLoop, calls=%fused_computation.26 | loop fusion | bytes 393216 | tf_op jit(solution)/shard_map/slice | solution.py:695
  2.3 4.5 %collective-permute-start = (bf16[192,256]{1,0:T(8,128)(2,1)}, bf16[192,256]{1,0:T(8,128)(2,1)S(1)}, u32[]{:S(2)}, u32[]{:S(2)}) collective-permute-start(bf16[192,256]{1,0:T(8,128)(2,1)} %bitcast.6), channel_id=1, source_target_pairs={{0,1},{1,2},{2,3},{3,4},{4,5},{5,6},{6,7},{8,9},{9,10},{10,11},{11... | collective-permute-start | bytes 294920 | tf_op jit(solution)/shard_map/ppermute | solution.py:545
  6.8 1.9 %collective-permute-start.1 = (bf16[192,256]{1,0:T(8,128)(2,1)}, bf16[192,256]{1,0:T(8,128)(2,1)S(1)}, u32[]{:S(2)}, u32[]{:S(2)}) collective-permute-start(bf16[192,256]{1,0:T(8,128)(2,1)} %bitcast.7), channel_id=1, source_target_pairs={{1,0},{2,1},{3,2},{4,3},{5,4},{6,5},{7,6},{9,8},{10,9},{11,10},{12... | collective-permute-start | bytes 294920 | tf_op jit(solution)/shard_map/ppermute | solution.py:545
  8.7 5.4 %teacher_moments.3 = (bf16[32,4224]{1,0:T(8,128)(2,1)}, bf16[32,4224]{1,0:T(8,128)(2,1)}) custom-call(bf16[4,128,4096]{2,1,0:T(8,128)(2,1)} %logit_hbm.3), custom_call_target="tpu_custom_call" | custom-call | flops 1500000000 | bytes 2600000 | tf_op jit(solution)/shard_map/teacher_moments/pallas_call | solution.py:111
  14.1 3.4 %collective-permute-start.2 = (bf16[32,4224]{1,0:T(8,128)(2,1)}, bf16[32,4224]{1,0:T(8,128)(2,1)S(1)}, u32[]{:S(2)}, u32[]{:S(2)}) collective-permute-start(bf16[32,4224]{1,0:T(8,128)(2,1)} %get-tuple-element.53), channel_id=1, source_target_pairs={{0,24},{8,16},{16,8},{24,0},{1,25},{9,17},{17,9},{25,1},{2,26},{10... | collective-permute-start | bytes 811016 | tf_op jit(solution)/shard_map/ppermute | solution.py:550
  17.5 5.5 %teacher_moments.2 = (bf16[32,4224]{1,0:T(8,128)(2,1)}, bf16[32,4224]{1,0:T(8,128)(2,1)}) custom-call(bf16[4,128,4096]{2,1,0:T(8,128)(2,1)} %logit_hbm.3), custom_call_target="tpu_custom_call" | custom-call | flops 1500000000 | bytes 2600000 | tf_op jit(solution)/shard_map/teacher_moments/pallas_call | solution.py:111
  25.9 9.1 %student_forward.1 = (bf16[2304,256]{1,0:T(8,128)(2,1)S(1)}, bf16[2048,256]{1,0:T(8,128)(2,1)S(1)}, f32[1024,128]{1,0:T(8,128)S(1)}, f32[1024,128]{1,0:T(8,128)S(1)}, f32[32,128]{1,0:T(8,128)S(1)}) custom-call(s32[6]{0:T(128)S(1)} %stack.35.place_ref.where_ref, bf16[192,256]{1,0:T(8,128)(2,1)S(1)} %collective-permute-done.before_ref, ...), custom_call_target="tpu_custom_call" | custom-call | flops 6000000000 | bytes 12000000 | tf_op jit(solution)/shard_map/student_forward/pallas_call | solution.py:278
  35.1 2.6 %turn.1 = (bf16[768,2176]{1,0:T(8,128)(2,1)S(1)}, bf16[768,2304]{1,0:T(8,128)(2,1)S(1)}, bf16[256,2048]{1,0:T(8,128)(2,1)S(1)}, bf16[3,768,256]{2,1,0:T(8,128)(2,1)S(1)}) custom-call(bf16[192,256]{1,0:T(8,128)(2,1)S(1)} %collective-permute-done.before_ref, bf16[2048,256]{1,0:T(8,128)(2,1)S(1)} %bitcast.23, ...), custom_call_target="tpu_custom_call" | custom-call | flops 3000000000 | bytes 14000000 | tf_op jit(solution)/shard_map/turn/pallas_call | solution.py:336
  37.7 1.8 %collective-permute-done.3.refs_1_ = bf16[32,4224]{1,0:T(8,128)(2,1)S(1)} collective-permute-done((bf16[32,4224]{1,0:T(8,128)(2,1)}, bf16[32,4224]{1,0:T(8,128)(2,1)S(1)}, u32[]{:S(2)}, u32[]{:S(2)}) %collective-permute-start.3) | collective-permute-done | bytes 270368 | tf_op jit(solution)/shard_map/ppermute | solution.py:550
  40.9 2.0 %collective-permute-start.5 = (bf16[16,4352]{1,0:T(8,128)(2,1)S(1)}, bf16[16,4352]{1,0:T(8,128)(2,1)S(1)}, u32[]{:S(2)}, u32[]{:S(2)}) collective-permute-start(bf16[16,4352]{1,0:T(8,128)(2,1)S(1)} %get-tuple-element.57), channel_id=1, source_target_pairs={{0,2},{2,0},{4,6},{6,4},{1,3},{3,1},{5,7},{7,5},{8,10},{10,8},{12,... | collective-permute-start | bytes 417800 | tf_op jit(solution)/shard_map/ppermute | solution.py:550
  45.4 2.2 %collective-permute-done.6.refs_2_ = bf16[16,4352]{1,0:T(8,128)(2,1)S(1)} collective-permute-done((bf16[16,4352]{1,0:T(8,128)(2,1)S(1)}, bf16[16,4352]{1,0:T(8,128)(2,1)S(1)}, u32[]{:S(2)}, u32[]{:S(2)}) %collective-permute-start.6) | collective-permute-done | bytes 139296 | tf_op jit(solution)/shard_map/ppermute | solution.py:550
  49.2 3.0 %collective-permute-start.8 = (bf16[32,4352]{1,0:T(8,128)(2,1)S(1)}, bf16[32,4352]{1,0:T(8,128)(2,1)S(1)}, u32[]{:S(2)}, u32[]{:S(2)}) collective-permute-start(bf16[32,4352]{1,0:T(8,128)(2,1)S(1)} %pad_maximum_fusion), channel_id=1, source_target_pairs={{0,1},{1,0},{2,3},{3,2},{4,5},{5,4},{6,7},{7,6},{8,9},{9,8},{10,11... | collective-permute-start | bytes 835592 | tf_op jit(solution)/shard_map/ppermute | solution.py:550
  53.4 1.8 %head_step.1 = (bf16[2048,256]{1,0:T(8,128)(2,1)S(1)}, bf16[128,256]{1,0:T(8,128)(2,1)S(1)}, bf16[128,256]{1,0:T(8,128)(2,1)S(1)}, f32[288,128]{1,0:T(8,128)S(1)}) custom-call(f32[1024,128]{1,0:T(8,128)S(1)} %get-tuple-element.47.log_ref, f32[1024,128]{1,0:T(8,128)S(1)} %get-tuple-element.48.base_ref, f32[32,128]{1,0:T(8,128)S(1)} %get-tuple-element.49.label_sum_ref, ...), custom_call_target="tpu_custom_call" | custom-call | flops 400000000 | bytes 5000000 | tf_op jit(solution)/shard_map/head_step/pallas_call | solution.py:404
  55.1 2.3 %collective-permute-start.10 = (bf16[128,256]{1,0:T(8,128)(2,1)S(1)}, bf16[128,256]{1,0:T(8,128)(2,1)S(1)}, u32[]{:S(2)}, u32[]{:S(2)}) collective-permute-start(bf16[128,256]{1,0:T(8,128)(2,1)S(1)} %get-tuple-element.61), channel_id=1, source_target_pairs={{1,0},{2,1},{3,2},{4,3},{5,4},{6,5},{7,6},{9,8},{10,9},{11,10},{12... | collective-permute-start | bytes 196616 | tf_op jit(solution)/shard_map/ppermute | solution.py:545
  57.4 3.3 %collective-permute-start.9 = (bf16[128,256]{1,0:T(8,128)(2,1)S(1)}, bf16[128,256]{1,0:T(8,128)(2,1)S(1)}, u32[]{:S(2)}, u32[]{:S(2)}) collective-permute-start(bf16[128,256]{1,0:T(8,128)(2,1)S(1)} %get-tuple-element.60), channel_id=1, source_target_pairs={{0,1},{1,2},{2,3},{3,4},{4,5},{5,6},{6,7},{8,9},{9,10},{10,11},{11... | collective-permute-start | bytes 196616 | tf_op jit(solution)/shard_map/ppermute | solution.py:545
  60.7 4.5 %second_step.1 = (bf16[2304,256]{1,0:T(8,128)(2,1)S(1)}, bf16[1536,256]{1,0:T(8,128)(2,1)S(1)}) custom-call(bf16[768,2304]{1,0:T(8,128)(2,1)S(1)} %get-tuple-element.64.ht_ref, bf16[2048,256]{1,0:T(8,128)(2,1)S(1)} %get-tuple-element.62.grad_ref, bf16[3,768,256]{2,1,0:T(8,128)(2,1)S(1)} %get-tuple-element.65.wt_ref.refs_0_, ...), custom_call_target="tpu_custom_call" | custom-call | flops 4499999744 | bytes 9000000 | tf_op jit(solution)/shard_map/second_step/pallas_call | solution.py:449
  65.3 4.7 %first_step.1 = (bf16[416,256]{1,0:T(8,128)(2,1)S(1)}, bf16[416,256]{1,0:T(8,128)(2,1)S(1)}, bf16[416,256]{1,0:T(8,128)(2,1)S(1)}, bf16[416,256]{1,0:T(8,128)(2,...) custom-call(s32[6]{0:T(128)S(1)} %stack.35.place_ref.where_ref, ...), custom_call_target="tpu_custom_call" | custom-call | flops 5000000000 | bytes 10000000 | tf_op jit(solution)/shard_map/first_step/pallas_call | solution.py:522
  73.6 1.8 %collective-permute-start.17 = (bf16[416,256]{1,0:T(8,128)(2,1)S(1)}, bf16[416,256]{1,0:T(8,128)(2,1)S(1)}, u32[]{:S(2)}, u32[]{:S(2)}) collective-permute-start(bf16[416,256]{1,0:T(8,128)(2,1)S(1)} %add_convert_fusion), channel_id=1, source_target_pairs={{0,6},{2,4},{4,2},{6,0},{1,7},{3,5},{5,3},{7,1},{8,14},{10,12},{12... | collective-permute-start | bytes 638984 | tf_op jit(solution)/shard_map/ppermute | solution.py:550
  75.6 2.3 %collective-permute-start.26 = (bf16[192,256]{1,0:T(8,128)(2,1)S(1)}, bf16[192,256]{1,0:T(8,128)(2,1)S(1)}, u32[]{:S(2)}, u32[]{:S(2)}) collective-permute-start(bf16[192,256]{1,0:T(8,128)(2,1)S(1)} %get-tuple-element.95), channel_id=1, source_target_pairs={{0,16},{8,24},{16,0},{24,8},{1,17},{9,25},{17,1},{25,9},{2,18},{10... | collective-permute-start | bytes 294920 | tf_op jit(solution)/shard_map/ppermute | solution.py:550
  78.3 2.1 %collective-permute-start.27 = (bf16[192,256]{1,0:T(8,128)(2,1)S(1)}, bf16[192,256]{1,0:T(8,128)(2,1)S(1)}, u32[]{:S(2)}, u32[]{:S(2)}) collective-permute-start(bf16[192,256]{1,0:T(8,128)(2,1)S(1)} %get-tuple-element.94), channel_id=1, source_target_pairs={{0,24},{8,16},{16,8},{24,0},{1,25},{9,17},{17,9},{25,1},{2,26},{10... | collective-permute-start | bytes 294920 | tf_op jit(solution)/shard_map/ppermute | solution.py:550
  80.3 3.0 %collective-permute-done.17 = bf16[416,256]{1,0:T(8,128)(2,1)S(1)} collective-permute-done((bf16[416,256]{1,0:T(8,128)(2,1)S(1)}, bf16[416,256]{1,0:T(8,128)(2,1)S(1)}, u32[]{:S(2)}, u32[]{:S(2)}) %collective-permute-start.17) | collective-permute-done | bytes 213024 | tf_op jit(solution)/shard_map/ppermute | solution.py:550
  83.5 2.5 %collective-permute-start.19 = (bf16[104,256]{1,0:T(8,128)(2,1)S(1)}, bf16[104,256]{1,0:T(8,128)(2,1)S(1)}, u32[]{:S(2)}, u32[]{:S(2)}) collective-permute-start(bf16[104,256]{1,0:T(8,128)(2,1)S(1)} %get-tuple-element.92), channel_id=1, source_target_pairs={{0,16},{8,24},{16,0},{24,8},{1,17},{9,25},{17,1},{25,9},{2,18},{10... | collective-permute-start | bytes 159752 | tf_op jit(solution)/shard_map/ppermute | solution.py:550
  87.1 2.0 %collective-permute-start.28 = (bf16[48,256]{1,0:T(8,128)(2,1)S(1)}, bf16[48,256]{1,0:T(8,128)(2,1)S(1)}, u32[]{:S(2)}, u32[]{:S(2)}) collective-permute-start(bf16[48,256]{1,0:T(8,128)(2,1)S(1)} %get-tuple-element.97), channel_id=1, source_target_pairs={{0,2},{2,0},{4,6},{6,4},{1,3},{3,1},{5,7},{7,5},{8,10},{10,8},{12,... | collective-permute-start | bytes 73736 | tf_op jit(solution)/shard_map/ppermute | solution.py:550
  91.2 1.7 %collective-permute-start.22 = (bf16[104,256]{1,0:T(8,128)(2,1)S(1)}, bf16[104,256]{1,0:T(8,128)(2,1)S(1)}, u32[]{:S(2)}, u32[]{:S(2)}) collective-permute-start(bf16[104,256]{1,0:T(8,128)(2,1)S(1)} %add_convert_fusion.8), channel_id=1, source_target_pairs={{0,16},{8,24},{16,0},{24,8},{1,17},{9,25},{17,1},{25,9},{2,18},{10... | collective-permute-start | bytes 159752 | tf_op jit(solution)/shard_map/ppermute | solution.py:550
  92.9 1.8 %collective-permute-start.23 = (bf16[104,256]{1,0:T(8,128)(2,1)S(1)}, bf16[104,256]{1,0:T(8,128)(2,1)S(1)}, u32[]{:S(2)}, u32[]{:S(2)}) collective-permute-start(bf16[104,256]{1,0:T(8,128)(2,1)S(1)} %add_convert_fusion.8), channel_id=1, source_target_pairs={{0,24},{8,16},{16,8},{24,0},{1,25},{9,17},{17,9},{25,1},{2,26},{10... | collective-permute-start | bytes 159752 | tf_op jit(solution)/shard_map/ppermute | solution.py:550
  94.7 2.0 %collective-permute-start.31 = (bf16[48,256]{1,0:T(8,128)(2,1)S(1)}, bf16[48,256]{1,0:T(8,128)(2,1)S(1)}, u32[]{:S(2)}, u32[]{:S(2)}) collective-permute-start(bf16[48,256]{1,0:T(8,128)(2,1)S(1)} %add_convert_fusion.13), channel_id=1, source_target_pairs={{0,2},{2,0},{4,6},{6,4},{1,3},{3,1},{5,7},{7,5},{8,10},{10,8},{12,... | collective-permute-start | bytes 73736 | tf_op jit(solution)/shard_map/ppermute | solution.py:550
  101.8 2.1 %collective-permute-start.43 = (bf16[192,256]{1,0:T(8,128)(2,1)S(1)}, bf16[192,256]{1,0:T(8,128)(2,1)S(1)}, u32[]{:S(2)}, u32[]{:S(2)}) collective-permute-start(bf16[192,256]{1,0:T(8,128)(2,1)S(1)} %pad_maximum_fusion.2), channel_id=1, source_target_pairs={{0,24},{8,16},{16,8},{24,0},{1,25},{9,17},{17,9},{25,1},{2,26},{10... | collective-permute-start | bytes 294920 | tf_op jit(solution)/shard_map/ppermute | solution.py:550
  107.1 6.8 %collective-permute-start.44 = (bf16[768,256]{1,0:T(8,128)(2,1)S(1)}, bf16[768,256]{1,0:T(8,128)(2,1)S(1)}, u32[]{:S(2)}, u32[]{:S(2)}) collective-permute-start(bf16[768,256]{1,0:T(8,128)(2,1)S(1)} %constant_dynamic-update-slice_fusion.refs_4_), channel_id=1, source_target_pairs={{0,1},{1,0},{2,3},{3,2},{4,5},{5,4},{6,7},{7,6},{8,9},{9,8},{10,11... | collective-permute-start | bytes 1179656 | tf_op jit(solution)/shard_map/ppermute | solution.py:550
  114.0 1.5 %collective-permute-start.36 = (bf16[416,256]{1,0:T(8,128)(2,1)S(1)}, bf16[416,256]{1,0:T(8,128)(2,1)S(1)}, u32[]{:S(2)}, u32[]{:S(2)}) collective-permute-start(bf16[416,256]{1,0:T(8,128)(2,1)S(1)} %collective-permute-done.35.refs_1_), channel_id=1, source_target_pairs={{0,1},{1,0},{2,3},{3,2},{4,5},{5,4},{6,7},{7,6},{8,9},{9,8},{10,11... | collective-permute-start | bytes 638984 | tf_op jit(solution)/shard_map/ppermute | solution.py:550
  115.5 2.4 %collective-permute-start.38 = (bf16[416,256]{1,0:T(8,128)(2,1)S(1)}, bf16[416,256]{1,0:T(8,128)(2,1)S(1)}, u32[]{:S(2)}, u32[]{:S(2)}) collective-permute-start(bf16[416,256]{1,0:T(8,128)(2,1)S(1)} %collective-permute-done.37.refs_2_), channel_id=1, source_target_pairs={{0,1},{1,0},{2,3},{3,2},{4,5},{5,4},{6,7},{7,6},{8,9},{9,8},{10,11... | collective-permute-start | bytes 638984 | tf_op jit(solution)/shard_map/ppermute | solution.py:550
  119.1 2.1 %assemble.2 = (f32[2304,256]{1,0:T(8,128)}, f32[2304,256]{1,0:T(8,128)}, f32[128,256]{1,0:T(8,128)S(1)}) custom-call(s32[6]{0:T(128)S(1)} %stack.35.place_ref.where_ref, bf16[416,256]{1,0:T(8,128)(2,1)S(1)} %pad_maximum_fusion.1.refs_0_, bf16[416,256]{1,0:T(8,128)(2,1)S(1)} %collective-permute-done.35.refs_1_, ...), custom_call_target="tpu_custom_call" | custom-call | flops 1000000 | bytes 3700000 | tf_op jit(solution)/shard_map/assemble/pallas_call | solution.py:619
  121.3 2.8 %assemble.3 = (f32[2304,256]{1,0:T(8,128)}, f32[2304,256]{1,0:T(8,128)}, f32[64,256]{1,0:T(8,128)}, f32[1,1]{1,0:T(1,128)}) custom-call(s32[6]{0:T(128)S(1)} %stack.35.place_ref.where_ref, bf16[416,256]{1,0:T(8,128)(2,1)S(1)} %collective-permute-done.34.refs_0_, ...), custom_call_target="tpu_custom_call", output_to_operand_aliasing={{0}: (6, {}), {1}: (7, {})} | custom-call | flops 1000000 | bytes 3700000 | tf_op jit(solution)/shard_map/assemble/pallas_call | solution.py:626
  (110 shorter events, 26.6 us)
Async XLA Ops:
  2.3 21.4 %collective-permute-start = (bf16[192,256]{1,0:T(8,128)(2,1)}, bf16[192,256]{1,0:T(8,128)(2,1)S(1)}, u32[]{:S(2)}, u32[]{:S(2)}) collective-permute-start(bf16[192,256]{1,0:T(8,128)(2,1)} %bitcast.6), channel_id=1, source_target_pairs={{0,1},{1,2},{2,3},{3,4},{4,5},{5,6},{6,7},{8,9},{9,10},{10,11},{11... | collective-permute-start | bytes 294920 | tf_op jit(solution)/shard_map/ppermute | solution.py:545
  6.8 16.9 %collective-permute-start.1 = (bf16[192,256]{1,0:T(8,128)(2,1)}, bf16[192,256]{1,0:T(8,128)(2,1)S(1)}, u32[]{:S(2)}, u32[]{:S(2)}) collective-permute-start(bf16[192,256]{1,0:T(8,128)(2,1)} %bitcast.7), channel_id=1, source_target_pairs={{1,0},{2,1},{3,2},{4,3},{5,4},{6,5},{7,6},{9,8},{10,9},{11,10},{12... | collective-permute-start | bytes 294920 | tf_op jit(solution)/shard_map/ppermute | solution.py:545
  14.1 23.6 %collective-permute-start.2 = (bf16[32,4224]{1,0:T(8,128)(2,1)}, bf16[32,4224]{1,0:T(8,128)(2,1)S(1)}, u32[]{:S(2)}, u32[]{:S(2)}) collective-permute-start(bf16[32,4224]{1,0:T(8,128)(2,1)} %get-tuple-element.53), channel_id=1, source_target_pairs={{0,24},{8,16},{16,8},{24,0},{1,25},{9,17},{17,9},{25,1},{2,26},{10... | collective-permute-start | bytes 811016 | tf_op jit(solution)/shard_map/ppermute | solution.py:550
  17.5 22.0 %collective-permute-start.3 = (bf16[32,4224]{1,0:T(8,128)(2,1)}, bf16[32,4224]{1,0:T(8,128)(2,1)S(1)}, u32[]{:S(2)}, u32[]{:S(2)}) collective-permute-start(bf16[32,4224]{1,0:T(8,128)(2,1)} %get-tuple-element.54), channel_id=1, source_target_pairs={{0,16},{8,24},{16,0},{24,8},{1,17},{9,25},{17,1},{25,9},{2,18},{10... | collective-permute-start | bytes 811016 | tf_op jit(solution)/shard_map/ppermute | solution.py:550
  23.0 16.5 %collective-permute-start.4 = (bf16[32,4224]{1,0:T(8,128)(2,1)}, bf16[32,4224]{1,0:T(8,128)(2,1)S(1)}, u32[]{:S(2)}, u32[]{:S(2)}) collective-permute-start(bf16[32,4224]{1,0:T(8,128)(2,1)} %get-tuple-element.55), channel_id=1, source_target_pairs={{0,8},{8,0},{16,24},{24,16},{1,9},{9,1},{17,25},{25,17},{2,10},{10... | collective-permute-start | bytes 811016 | tf_op jit(solution)/shard_map/ppermute | solution.py:550
  43.1 6.1 %collective-permute-start.7 = (bf16[16,4352]{1,0:T(8,128)(2,1)S(1)}, bf16[16,4352]{1,0:T(8,128)(2,1)S(1)}, u32[]{:S(2)}, u32[]{:S(2)}) collective-permute-start(bf16[16,4352]{1,0:T(8,128)(2,1)S(1)} %get-tuple-element.59), channel_id=1, source_target_pairs={{0,6},{2,4},{4,2},{6,0},{1,7},{3,5},{5,3},{7,1},{8,14},{10,12},{12... | collective-permute-start | bytes 417800 | tf_op jit(solution)/shard_map/ppermute | solution.py:550
  55.1 10.1 %collective-permute-start.10 = (bf16[128,256]{1,0:T(8,128)(2,1)S(1)}, bf16[128,256]{1,0:T(8,128)(2,1)S(1)}, u32[]{:S(2)}, u32[]{:S(2)}) collective-permute-start(bf16[128,256]{1,0:T(8,128)(2,1)S(1)} %get-tuple-element.61), channel_id=1, source_target_pairs={{1,0},{2,1},{3,2},{4,3},{5,4},{6,5},{7,6},{9,8},{10,9},{11,10},{12... | collective-permute-start | bytes 196616 | tf_op jit(solution)/shard_map/ppermute | solution.py:545
  57.4 7.8 %collective-permute-start.9 = (bf16[128,256]{1,0:T(8,128)(2,1)S(1)}, bf16[128,256]{1,0:T(8,128)(2,1)S(1)}, u32[]{:S(2)}, u32[]{:S(2)}) collective-permute-start(bf16[128,256]{1,0:T(8,128)(2,1)S(1)} %get-tuple-element.60), channel_id=1, source_target_pairs={{0,1},{1,2},{2,3},{3,4},{4,5},{5,6},{6,7},{8,9},{9,10},{10,11},{11... | collective-permute-start | bytes 196616 | tf_op jit(solution)/shard_map/ppermute | solution.py:545
  70.1 5.4 %collective-permute-start.24 = (bf16[768,256]{1,0:T(8,128)(2,1)S(1)}, bf16[768,256]{1,0:T(8,128)(2,1)S(1)}, u32[]{:S(2)}, u32[]{:S(2)}) collective-permute-start(bf16[768,256]{1,0:T(8,128)(2,1)S(1)} %get-tuple-element.78), channel_id=1, source_target_pairs={{0,1},{1,0},{2,3},{3,2},{4,5},{5,4},{6,7},{7,6},{8,9},{9,8},{10,11... | collective-permute-start | bytes 1179656 | tf_op jit(solution)/shard_map/ppermute | solution.py:550
  71.5 6.8 %collective-permute-start.13 = (bf16[416,256]{1,0:T(8,128)(2,1)S(1)}, bf16[416,256]{1,0:T(8,128)(2,1)S(1)}, u32[]{:S(2)}, u32[]{:S(2)}) collective-permute-start(bf16[416,256]{1,0:T(8,128)(2,1)S(1)} %add_convert_fusion.2), channel_id=1, source_target_pairs={{0,2},{2,0},{4,6},{6,4},{1,3},{3,1},{5,7},{7,5},{8,10},{10,8},{12,... | collective-permute-start | bytes 638984 | tf_op jit(solution)/shard_map/ppermute | solution.py:550
  72.9 7.4 %collective-permute-start.15 = (bf16[416,256]{1,0:T(8,128)(2,1)S(1)}, bf16[416,256]{1,0:T(8,128)(2,1)S(1)}, u32[]{:S(2)}, u32[]{:S(2)}) collective-permute-start(bf16[416,256]{1,0:T(8,128)(2,1)S(1)} %add_convert_fusion.1), channel_id=1, source_target_pairs={{0,4},{2,6},{4,0},{6,2},{1,5},{3,7},{5,1},{7,3},{8,12},{10,14},{12... | collective-permute-start | bytes 638984 | tf_op jit(solution)/shard_map/ppermute | solution.py:550
  73.6 9.8 %collective-permute-start.17 = (bf16[416,256]{1,0:T(8,128)(2,1)S(1)}, bf16[416,256]{1,0:T(8,128)(2,1)S(1)}, u32[]{:S(2)}, u32[]{:S(2)}) collective-permute-start(bf16[416,256]{1,0:T(8,128)(2,1)S(1)} %add_convert_fusion), channel_id=1, source_target_pairs={{0,6},{2,4},{4,2},{6,0},{1,7},{3,5},{5,3},{7,1},{8,14},{10,12},{12... | collective-permute-start | bytes 638984 | tf_op jit(solution)/shard_map/ppermute | solution.py:550
  75.6 10.4 %collective-permute-start.25 = (bf16[192,256]{1,0:T(8,128)(2,1)S(1)}, bf16[192,256]{1,0:T(8,128)(2,1)S(1)}, u32[]{:S(2)}, u32[]{:S(2)}) collective-permute-start(bf16[192,256]{1,0:T(8,128)(2,1)S(1)} %get-tuple-element.96), channel_id=1, source_target_pairs={{0,8},{8,0},{16,24},{24,16},{1,9},{9,1},{17,25},{25,17},{2,10},{10... | collective-permute-start | bytes 294920 | tf_op jit(solution)/shard_map/ppermute | solution.py:550
  75.6 11.4 %collective-permute-start.26 = (bf16[192,256]{1,0:T(8,128)(2,1)S(1)}, bf16[192,256]{1,0:T(8,128)(2,1)S(1)}, u32[]{:S(2)}, u32[]{:S(2)}) collective-permute-start(bf16[192,256]{1,0:T(8,128)(2,1)S(1)} %get-tuple-element.95), channel_id=1, source_target_pairs={{0,16},{8,24},{16,0},{24,8},{1,17},{9,25},{17,1},{25,9},{2,18},{10... | collective-permute-start | bytes 294920 | tf_op jit(solution)/shard_map/ppermute | solution.py:550
  78.3 8.8 %collective-permute-start.27 = (bf16[192,256]{1,0:T(8,128)(2,1)S(1)}, bf16[192,256]{1,0:T(8,128)(2,1)S(1)}, u32[]{:S(2)}, u32[]{:S(2)}) collective-permute-start(bf16[192,256]{1,0:T(8,128)(2,1)S(1)} %get-tuple-element.94), channel_id=1, source_target_pairs={{0,24},{8,16},{16,8},{24,0},{1,25},{9,17},{17,9},{25,1},{2,26},{10... | collective-permute-start | bytes 294920 | tf_op jit(solution)/shard_map/ppermute | solution.py:550
  83.4 5.7 %collective-permute-start.18 = (bf16[104,256]{1,0:T(8,128)(2,1)S(1)}, bf16[104,256]{1,0:T(8,128)(2,1)S(1)}, u32[]{:S(2)}, u32[]{:S(2)}) collective-permute-start(bf16[104,256]{1,0:T(8,128)(2,1)S(1)} %get-tuple-element.90), channel_id=1, source_target_pairs={{0,8},{8,0},{16,24},{24,16},{1,9},{9,1},{17,25},{25,17},{2,10},{10... | collective-permute-start | bytes 159752 | tf_op jit(solution)/shard_map/ppermute | solution.py:550
  83.5 6.8 %collective-permute-start.19 = (bf16[104,256]{1,0:T(8,128)(2,1)S(1)}, bf16[104,256]{1,0:T(8,128)(2,1)S(1)}, u32[]{:S(2)}, u32[]{:S(2)}) collective-permute-start(bf16[104,256]{1,0:T(8,128)(2,1)S(1)} %get-tuple-element.92), channel_id=1, source_target_pairs={{0,16},{8,24},{16,0},{24,8},{1,17},{9,25},{17,1},{25,9},{2,18},{10... | collective-permute-start | bytes 159752 | tf_op jit(solution)/shard_map/ppermute | solution.py:550
  87.1 5.7 %collective-permute-start.28 = (bf16[48,256]{1,0:T(8,128)(2,1)S(1)}, bf16[48,256]{1,0:T(8,128)(2,1)S(1)}, u32[]{:S(2)}, u32[]{:S(2)}) collective-permute-start(bf16[48,256]{1,0:T(8,128)(2,1)S(1)} %get-tuple-element.97), channel_id=1, source_target_pairs={{0,2},{2,0},{4,6},{6,4},{1,3},{3,1},{5,7},{7,5},{8,10},{10,8},{12,... | collective-permute-start | bytes 73736 | tf_op jit(solution)/shard_map/ppermute | solution.py:550
  89.1 5.6 %collective-permute-start.29 = (bf16[48,256]{1,0:T(8,128)(2,1)S(1)}, bf16[48,256]{1,0:T(8,128)(2,1)S(1)}, u32[]{:S(2)}, u32[]{:S(2)}) collective-permute-start(bf16[48,256]{1,0:T(8,128)(2,1)S(1)} %get-tuple-element.99), channel_id=1, source_target_pairs={{0,4},{2,6},{4,0},{6,2},{1,5},{3,7},{5,1},{7,3},{8,12},{10,14},{12... | collective-permute-start | bytes 73736 | tf_op jit(solution)/shard_map/ppermute | solution.py:550
  89.2 5.5 %collective-permute-start.30 = (bf16[48,256]{1,0:T(8,128)(2,1)S(1)}, bf16[48,256]{1,0:T(8,128)(2,1)S(1)}, u32[]{:S(2)}, u32[]{:S(2)}) collective-permute-start(bf16[48,256]{1,0:T(8,128)(2,1)S(1)} %get-tuple-element.98), channel_id=1, source_target_pairs={{0,6},{2,4},{4,2},{6,0},{1,7},{3,5},{5,3},{7,1},{8,14},{10,12},{12... | collective-permute-start | bytes 73736 | tf_op jit(solution)/shard_map/ppermute | solution.py:550
  91.1 5.6 %collective-permute-start.21 = (bf16[104,256]{1,0:T(8,128)(2,1)S(1)}, bf16[104,256]{1,0:T(8,128)(2,1)S(1)}, u32[]{:S(2)}, u32[]{:S(2)}) collective-permute-start(bf16[104,256]{1,0:T(8,128)(2,1)S(1)} %add_convert_fusion.8), channel_id=1, source_target_pairs={{0,8},{8,0},{16,24},{24,16},{1,9},{9,1},{17,25},{25,17},{2,10},{10... | collective-permute-start | bytes 159752 | tf_op jit(solution)/shard_map/ppermute | solution.py:550
  91.2 6.8 %collective-permute-start.22 = (bf16[104,256]{1,0:T(8,128)(2,1)S(1)}, bf16[104,256]{1,0:T(8,128)(2,1)S(1)}, u32[]{:S(2)}, u32[]{:S(2)}) collective-permute-start(bf16[104,256]{1,0:T(8,128)(2,1)S(1)} %add_convert_fusion.8), channel_id=1, source_target_pairs={{0,16},{8,24},{16,0},{24,8},{1,17},{9,25},{17,1},{25,9},{2,18},{10... | collective-permute-start | bytes 159752 | tf_op jit(solution)/shard_map/ppermute | solution.py:550
  100.3 5.4 %collective-permute-start.41 = (bf16[192,256]{1,0:T(8,128)(2,1)S(1)}, bf16[192,256]{1,0:T(8,128)(2,1)S(1)}, u32[]{:S(2)}, u32[]{:S(2)}) collective-permute-start(bf16[192,256]{1,0:T(8,128)(2,1)S(1)} %pad_maximum_fusion.2), channel_id=1, source_target_pairs={{0,8},{8,0},{16,24},{24,16},{1,9},{9,1},{17,25},{25,17},{2,10},{10... | collective-permute-start | bytes 294920 | tf_op jit(solution)/shard_map/ppermute | solution.py:550
  100.4 6.6 %collective-permute-start.42 = (bf16[192,256]{1,0:T(8,128)(2,1)S(1)}, bf16[192,256]{1,0:T(8,128)(2,1)S(1)}, u32[]{:S(2)}, u32[]{:S(2)}) collective-permute-start(bf16[192,256]{1,0:T(8,128)(2,1)S(1)} %pad_maximum_fusion.2), channel_id=1, source_target_pairs={{0,16},{8,24},{16,0},{24,8},{1,17},{9,25},{17,1},{25,9},{2,18},{10... | collective-permute-start | bytes 294920 | tf_op jit(solution)/shard_map/ppermute | solution.py:550
  101.8 5.3 %collective-permute-start.43 = (bf16[192,256]{1,0:T(8,128)(2,1)S(1)}, bf16[192,256]{1,0:T(8,128)(2,1)S(1)}, u32[]{:S(2)}, u32[]{:S(2)}) collective-permute-start(bf16[192,256]{1,0:T(8,128)(2,1)S(1)} %pad_maximum_fusion.2), channel_id=1, source_target_pairs={{0,24},{8,16},{16,8},{24,0},{1,25},{9,17},{17,9},{25,1},{2,26},{10... | collective-permute-start | bytes 294920 | tf_op jit(solution)/shard_map/ppermute | solution.py:550
  103.9 10.1 %collective-permute-start.35 = (bf16[416,256]{1,0:T(8,128)(2,1)S(1)}, bf16[416,256]{1,0:T(8,128)(2,1)S(1)}, u32[]{:S(2)}, u32[]{:S(2)}) collective-permute-start(bf16[416,256]{1,0:T(8,128)(2,1)S(1)} %pad_maximum_fusion.1.refs_0_), channel_id=1, source_target_pairs={{0,2},{2,0},{4,6},{6,4},{1,3},{3,1},{5,7},{7,5},{8,10},{10,8},{12,... | collective-permute-start | bytes 638984 | tf_op jit(solution)/shard_map/ppermute | solution.py:550
  104.8 10.7 %collective-permute-start.37 = (bf16[416,256]{1,0:T(8,128)(2,1)S(1)}, bf16[416,256]{1,0:T(8,128)(2,1)S(1)}, u32[]{:S(2)}, u32[]{:S(2)}) collective-permute-start(bf16[416,256]{1,0:T(8,128)(2,1)S(1)} %pad_maximum_fusion.1.refs_0_), channel_id=1, source_target_pairs={{0,4},{2,6},{4,0},{6,2},{1,5},{3,7},{5,1},{7,3},{8,12},{10,14},{12... | collective-permute-start | bytes 638984 | tf_op jit(solution)/shard_map/ppermute | solution.py:550
  105.7 12.2 %collective-permute-start.39 = (bf16[416,256]{1,0:T(8,128)(2,1)S(1)}, bf16[416,256]{1,0:T(8,128)(2,1)S(1)}, u32[]{:S(2)}, u32[]{:S(2)}) collective-permute-start(bf16[416,256]{1,0:T(8,128)(2,1)S(1)} %pad_maximum_fusion.1.refs_0_), channel_id=1, source_target_pairs={{0,6},{2,4},{4,2},{6,0},{1,7},{3,5},{5,3},{7,1},{8,14},{10,12},{12... | collective-permute-start | bytes 638984 | tf_op jit(solution)/shard_map/ppermute | solution.py:550
  107.1 14.1 %collective-permute-start.44 = (bf16[768,256]{1,0:T(8,128)(2,1)S(1)}, bf16[768,256]{1,0:T(8,128)(2,1)S(1)}, u32[]{:S(2)}, u32[]{:S(2)}) collective-permute-start(bf16[768,256]{1,0:T(8,128)(2,1)S(1)} %constant_dynamic-update-slice_fusion.refs_4_), channel_id=1, source_target_pairs={{0,1},{1,0},{2,3},{3,2},{4,5},{5,4},{6,7},{7,6},{8,9},{9,8},{10,11... | collective-permute-start | bytes 1179656 | tf_op jit(solution)/shard_map/ppermute | solution.py:550
  113.9 7.3 %collective-permute-start.34 = (bf16[416,256]{1,0:T(8,128)(2,1)S(1)}, bf16[416,256]{1,0:T(8,128)(2,1)S(1)}, u32[]{:S(2)}, u32[]{:S(2)}) collective-permute-start(bf16[416,256]{1,0:T(8,128)(2,1)S(1)} %pad_maximum_fusion.1.refs_0_), channel_id=1, source_target_pairs={{0,1},{1,0},{2,3},{3,2},{4,5},{5,4},{6,7},{7,6},{8,9},{9,8},{10,11... | collective-permute-start | bytes 638984 | tf_op jit(solution)/shard_map/ppermute | solution.py:550
  114.0 7.3 %collective-permute-start.36 = (bf16[416,256]{1,0:T(8,128)(2,1)S(1)}, bf16[416,256]{1,0:T(8,128)(2,1)S(1)}, u32[]{:S(2)}, u32[]{:S(2)}) collective-permute-start(bf16[416,256]{1,0:T(8,128)(2,1)S(1)} %collective-permute-done.35.refs_1_), channel_id=1, source_target_pairs={{0,1},{1,0},{2,3},{3,2},{4,5},{5,4},{6,7},{7,6},{8,9},{9,8},{10,11... | collective-permute-start | bytes 638984 | tf_op jit(solution)/shard_map/ppermute | solution.py:550
  115.5 5.7 %collective-permute-start.38 = (bf16[416,256]{1,0:T(8,128)(2,1)S(1)}, bf16[416,256]{1,0:T(8,128)(2,1)S(1)}, u32[]{:S(2)}, u32[]{:S(2)}) collective-permute-start(bf16[416,256]{1,0:T(8,128)(2,1)S(1)} %collective-permute-done.37.refs_2_), channel_id=1, source_target_pairs={{0,1},{1,0},{2,3},{3,2},{4,5},{5,4},{6,7},{7,6},{8,9},{9,8},{10,11... | collective-permute-start | bytes 638984 | tf_op jit(solution)/shard_map/ppermute | solution.py:550
  (21 other events, 89.7 us)
where the time goes:
time: 125 us; the launch traced here: 124 us
  starting transfers between devices  63.6 us (51%)
  Pallas kernels  39.8 us (32%)
  waiting for transfers between devices  14.6 us (12%)
  local copies, waits for them, and re-layouts  4.32 us (3%)
  between operations  1.25 us (1%)
    ppermute x41, starting transfers between devices, pairwise(): return lax.ppermute(array, axis, [(i, i ^ step) for i in range(count)])  51.6 us
    ppermute x41, waiting for transfers between devices, pairwise(): return lax.ppermute(array, axis, [(i, i ^ step) for i in range(count)])  14.6 us
    ppermute x4, starting transfers between devices, neighbours(): return (lax.ppermute(last, axis, up), lax.ppermute(first, axis, down))  12 us
    pallas_call x2, Pallas kernels, teacher_moments(): pl.pallas_call(functools.partial(teacher_kernel, classes, flip), in_specs...  10.8 us
    pallas_call x1, Pallas kernels, student_forward(): pl.pallas_call(functools.partial(student_kernel, width), in_specs=[scalar...  9.11 us
    pallas_call x1, Pallas kernels, first_step(): pl.pallas_call(functools.partial(first_kernel, width, plan), in_specs=[sc...  4.65 us
    pallas_call x1, Pallas kernels, second_step(): pl.pallas_call(functools.partial(second_kernel, width), in_specs=whole(4)...  4.51 us
    pallas_call x1, Pallas kernels, assemble(): pl.pallas_call(kernel, in_specs=[scalars(), *whole(count), *hbm(2), *whol...  2.77 us
  transfers between devices with their start and end apart: 45, of which 13 were waited for; matrix products, arithmetic and copies ran while one was open for 1% of the time, Pallas kernels for 23%

commit v1 on v0

--- a/solution.py
+++ b/solution.py
@@ -69,17 +69,22 @@
     same = (iota((MXU, MXU), 0) // classes == iota((MXU, MXU), 1) // classes).astype(BF16)
     acc_ref[...] = jnp.zeros_like(acc_ref)
 
+    def group_sums(values):
+        rows = values[0].shape[0]
+        stacked = dot(jnp.concatenate([one.astype(BF16) for one in values], axis=0), same)
+        return [stacked[n * rows : (n + 1) * rows] for n in range(len(values))]
+
     @pl.loop(0, quarters)
     def _(i):
         pltpu.make_async_copy(logit_hbm.at[:, tile_rows, pl.ds(0, width)], x_ref.at[i], sems.at[i]).wait()
         each = range(parts)
         x = [x_ref[i, :, :, n * MXU : (n + 1) * MXU].astype(F32).reshape(members * tiles, MXU) for n in each]
         root = [jnp.exp(one * 0.25) for one in x]
-        total = [dot(one.astype(BF16), same) for one in root]
+        total = group_sums(root)
         root = [one * pl.reciprocal(whole_sum, approx=True) for one, whole_sum in zip(root, total)]
         square = [one * one for one in root]
         power = [one * one for one in square]
-        total = [dot(one.astype(BF16), same) for one in power]
+        total = group_sums(power)
         inverse = [pl.reciprocal(one, approx=True) for one in total]
         inverse = [one * (2.0 - whole_sum * one) for one, whole_sum in zip(inverse, total)]
         probs = [(one * other).reshape(members, tiles, MXU) for one, other in zip(power, inverse)]
@@ -88,7 +93,8 @@
             functools.reduce(jnp.add, [one[m] * one[m] for m in range(members)]) - sums * sums * (1.0 / members)
             for one, sums in zip(probs, first)
         ]
-        sums = [class_sums(one, classes) for one in within]
+        sums = class_sums(jnp.concatenate(within, axis=0), classes)
+        sums = [sums[n * tiles : (n + 1) * tiles] for n in each]
         acc = acc_ref[...]
         for n in each:
             acc = jnp.where(iota(acc.shape, 1) % 64 // per == i * parts + n, sums[n], acc)

time: 125 us -> 125 us (level)
  no operation moved by 1% of the time
where the time goes in v1:
time: 125 us; the launch traced here: 124 us
  starting transfers between devices  63.6 us (51%)
  Pallas kernels  39.8 us (32%)
  waiting for transfers between devices  14.7 us (12%)
  local copies, waits for them, and re-layouts  4.32 us (3%)
  between operations  1.25 us (1%)
    ppermute x41, starting transfers between devices, pairwise(): return lax.ppermute(array, axis, [(i, i ^ step) for i in range(count)])  51.6 us
    ppermute x41, waiting for transfers between devices, pairwise(): return lax.ppermute(array, axis, [(i, i ^ step) for i in range(count)])  14.7 us
    ppermute x4, starting transfers between devices, neighbours(): return (lax.ppermute(last, axis, up), lax.ppermute(first, axis, down))  12 us
    pallas_call x2, Pallas kernels, teacher_moments(): pl.pallas_call(functools.partial(teacher_kernel, classes, flip), in_specs...  10.8 us
    pallas_call x1, Pallas kernels, student_forward(): pl.pallas_call(functools.partial(student_kernel, width), in_specs=[scalar...  9.12 us
    pallas_call x1, Pallas kernels, first_step(): pl.pallas_call(functools.partial(first_kernel, width, plan), in_specs=[sc...  4.65 us
    pallas_call x1, Pallas kernels, second_step(): pl.pallas_call(functools.partial(second_kernel, width), in_specs=whole(4)...  4.51 us
    pallas_call x1, Pallas kernels, assemble(): pl.pallas_call(kernel, in_specs=[scalars(), *whole(count), *hbm(2), *whol...  2.77 us
  transfers between devices with their start and end apart: 45, of which 13 were waited for; matrix products, arithmetic and copies ran while one was open for 1% of the time, Pallas kernels for 23%

profile of v1, /device:TPU:1, one launch (start us, length us, event | category | flops | bytes accessed | tf_op | source)
XLA Modules:
  0.0 124.2 jit_solution(12973521407605360718)
XLA Ops:
  0.6 1.6 %fusion = (bf16[1,3,64,256]{3,2,1,0:T(8,128)(2,1)}, bf16[1,3,64,256]{3,2,1,0:T(8,128)(2,1)}) fusion(bf16[1,32,64,256]{3,2,1,0:T(8,128)(2,1)} %param.9), kind=kLoop, calls=%fused_computation.26 | loop fusion | bytes 393216 | tf_op jit(solution)/shard_map/slice | solution.py:701
  2.3 4.5 %collective-permute-start = (bf16[192,256]{1,0:T(8,128)(2,1)}, bf16[192,256]{1,0:T(8,128)(2,1)S(1)}, u32[]{:S(2)}, u32[]{:S(2)}) collective-permute-start(bf16[192,256]{1,0:T(8,128)(2,1)} %bitcast.6), channel_id=1, source_target_pairs={{0,1},{1,2},{2,3},{3,4},{4,5},{5,6},{6,7},{8,9},{9,10},{10,11},{11... | collective-permute-start | bytes 294920 | tf_op jit(solution)/shard_map/ppermute | solution.py:551
  6.8 1.9 %collective-permute-start.1 = (bf16[192,256]{1,0:T(8,128)(2,1)}, bf16[192,256]{1,0:T(8,128)(2,1)S(1)}, u32[]{:S(2)}, u32[]{:S(2)}) collective-permute-start(bf16[192,256]{1,0:T(8,128)(2,1)} %bitcast.7), channel_id=1, source_target_pairs={{1,0},{2,1},{3,2},{4,3},{5,4},{6,5},{7,6},{9,8},{10,9},{11,10},{12... | collective-permute-start | bytes 294920 | tf_op jit(solution)/shard_map/ppermute | solution.py:551
  8.7 5.3 %teacher_moments.3 = (bf16[32,4224]{1,0:T(8,128)(2,1)}, bf16[32,4224]{1,0:T(8,128)(2,1)}) custom-call(bf16[4,128,4096]{2,1,0:T(8,128)(2,1)} %logit_hbm.3), custom_call_target="tpu_custom_call" | custom-call | flops 1500000000 | bytes 2600000 | tf_op jit(solution)/shard_map/teacher_moments/pallas_call | solution.py:117
  14.0 3.4 %collective-permute-start.2 = (bf16[32,4224]{1,0:T(8,128)(2,1)}, bf16[32,4224]{1,0:T(8,128)(2,1)S(1)}, u32[]{:S(2)}, u32[]{:S(2)}) collective-permute-start(bf16[32,4224]{1,0:T(8,128)(2,1)} %get-tuple-element.53), channel_id=1, source_target_pairs={{0,24},{8,16},{16,8},{24,0},{1,25},{9,17},{17,9},{25,1},{2,26},{10... | collective-permute-start | bytes 811016 | tf_op jit(solution)/shard_map/ppermute | solution.py:556
  17.5 5.4 %teacher_moments.2 = (bf16[32,4224]{1,0:T(8,128)(2,1)}, bf16[32,4224]{1,0:T(8,128)(2,1)}) custom-call(bf16[4,128,4096]{2,1,0:T(8,128)(2,1)} %logit_hbm.3), custom_call_target="tpu_custom_call" | custom-call | flops 1500000000 | bytes 2600000 | tf_op jit(solution)/shard_map/teacher_moments/pallas_call | solution.py:117
  25.9 9.1 %student_forward.1 = (bf16[2304,256]{1,0:T(8,128)(2,1)S(1)}, bf16[2048,256]{1,0:T(8,128)(2,1)S(1)}, f32[1024,128]{1,0:T(8,128)S(1)}, f32[1024,128]{1,0:T(8,128)S(1)}, f32[32,128]{1,0:T(8,128)S(1)}) custom-call(s32[6]{0:T(128)S(1)} %stack.35.place_ref.where_ref, bf16[192,256]{1,0:T(8,128)(2,1)S(1)} %collective-permute-done.before_ref, ...), custom_call_target="tpu_custom_call" | custom-call | flops 6000000000 | bytes 12000000 | tf_op jit(solution)/shard_map/student_forward/pallas_call | solution.py:284
  35.0 2.6 %turn.1 = (bf16[768,2176]{1,0:T(8,128)(2,1)S(1)}, bf16[768,2304]{1,0:T(8,128)(2,1)S(1)}, bf16[256,2048]{1,0:T(8,128)(2,1)S(1)}, bf16[3,768,256]{2,1,0:T(8,128)(2,1)S(1)}) custom-call(bf16[192,256]{1,0:T(8,128)(2,1)S(1)} %collective-permute-done.before_ref, bf16[2048,256]{1,0:T(8,128)(2,1)S(1)} %bitcast.23, ...), custom_call_target="tpu_custom_call" | custom-call | flops 3000000000 | bytes 14000000 | tf_op jit(solution)/shard_map/turn/pallas_call | solution.py:342
  37.7 1.8 %collective-permute-done.3.refs_1_ = bf16[32,4224]{1,0:T(8,128)(2,1)S(1)} collective-permute-done((bf16[32,4224]{1,0:T(8,128)(2,1)}, bf16[32,4224]{1,0:T(8,128)(2,1)S(1)}, u32[]{:S(2)}, u32[]{:S(2)}) %collective-permute-start.3) | collective-permute-done | bytes 270368 | tf_op jit(solution)/shard_map/ppermute | solution.py:556
  40.9 2.0 %collective-permute-start.5 = (bf16[16,4352]{1,0:T(8,128)(2,1)S(1)}, bf16[16,4352]{1,0:T(8,128)(2,1)S(1)}, u32[]{:S(2)}, u32[]{:S(2)}) collective-permute-start(bf16[16,4352]{1,0:T(8,128)(2,1)S(1)} %get-tuple-element.57), channel_id=1, source_target_pairs={{0,2},{2,0},{4,6},{6,4},{1,3},{3,1},{5,7},{7,5},{8,10},{10,8},{12,... | collective-permute-start | bytes 417800 | tf_op jit(solution)/shard_map/ppermute | solution.py:556
  45.4 2.2 %collective-permute-done.6.refs_2_ = bf16[16,4352]{1,0:T(8,128)(2,1)S(1)} collective-permute-done((bf16[16,4352]{1,0:T(8,128)(2,1)S(1)}, bf16[16,4352]{1,0:T(8,128)(2,1)S(1)}, u32[]{:S(2)}, u32[]{:S(2)}) %collective-permute-start.6) | collective-permute-done | bytes 139296 | tf_op jit(solution)/shard_map/ppermute | solution.py:556
  49.2 3.0 %collective-permute-start.8 = (bf16[32,4352]{1,0:T(8,128)(2,1)S(1)}, bf16[32,4352]{1,0:T(8,128)(2,1)S(1)}, u32[]{:S(2)}, u32[]{:S(2)}) collective-permute-start(bf16[32,4352]{1,0:T(8,128)(2,1)S(1)} %pad_maximum_fusion), channel_id=1, source_target_pairs={{0,1},{1,0},{2,3},{3,2},{4,5},{5,4},{6,7},{7,6},{8,9},{9,8},{10,11... | collective-permute-start | bytes 835592 | tf_op jit(solution)/shard_map/ppermute | solution.py:556
  53.3 1.8 %head_step.1 = (bf16[2048,256]{1,0:T(8,128)(2,1)S(1)}, bf16[128,256]{1,0:T(8,128)(2,1)S(1)}, bf16[128,256]{1,0:T(8,128)(2,1)S(1)}, f32[288,128]{1,0:T(8,128)S(1)}) custom-call(f32[1024,128]{1,0:T(8,128)S(1)} %get-tuple-element.47.log_ref, f32[1024,128]{1,0:T(8,128)S(1)} %get-tuple-element.48.base_ref, f32[32,128]{1,0:T(8,128)S(1)} %get-tuple-element.49.label_sum_ref, ...), custom_call_target="tpu_custom_call" | custom-call | flops 400000000 | bytes 5000000 | tf_op jit(solution)/shard_map/head_step/pallas_call | solution.py:410
  55.1 2.3 %collective-permute-start.10 = (bf16[128,256]{1,0:T(8,128)(2,1)S(1)}, bf16[128,256]{1,0:T(8,128)(2,1)S(1)}, u32[]{:S(2)}, u32[]{:S(2)}) collective-permute-start(bf16[128,256]{1,0:T(8,128)(2,1)S(1)} %get-tuple-element.61), channel_id=1, source_target_pairs={{1,0},{2,1},{3,2},{4,3},{5,4},{6,5},{7,6},{9,8},{10,9},{11,10},{12... | collective-permute-start | bytes 196616 | tf_op jit(solution)/shard_map/ppermute | solution.py:551
  57.4 3.3 %collective-permute-start.9 = (bf16[128,256]{1,0:T(8,128)(2,1)S(1)}, bf16[128,256]{1,0:T(8,128)(2,1)S(1)}, u32[]{:S(2)}, u32[]{:S(2)}) collective-permute-start(bf16[128,256]{1,0:T(8,128)(2,1)S(1)} %get-tuple-element.60), channel_id=1, source_target_pairs={{0,1},{1,2},{2,3},{3,4},{4,5},{5,6},{6,7},{8,9},{9,10},{10,11},{11... | collective-permute-start | bytes 196616 | tf_op jit(solution)/shard_map/ppermute | solution.py:551
  60.7 4.5 %second_step.1 = (bf16[2304,256]{1,0:T(8,128)(2,1)S(1)}, bf16[1536,256]{1,0:T(8,128)(2,1)S(1)}) custom-call(bf16[768,2304]{1,0:T(8,128)(2,1)S(1)} %get-tuple-element.64.ht_ref, bf16[2048,256]{1,0:T(8,128)(2,1)S(1)} %get-tuple-element.62.grad_ref, bf16[3,768,256]{2,1,0:T(8,128)(2,1)S(1)} %get-tuple-element.65.wt_ref.refs_0_, ...), custom_call_target="tpu_custom_call" | custom-call | flops 4499999744 | bytes 9000000 | tf_op jit(solution)/shard_map/second_step/pallas_call | solution.py:455
  65.2 4.7 %first_step.1 = (bf16[416,256]{1,0:T(8,128)(2,1)S(1)}, bf16[416,256]{1,0:T(8,128)(2,1)S(1)}, bf16[416,256]{1,0:T(8,128)(2,1)S(1)}, bf16[416,256]{1,0:T(8,128)(2,...) custom-call(s32[6]{0:T(128)S(1)} %stack.35.place_ref.where_ref, ...), custom_call_target="tpu_custom_call" | custom-call | flops 5000000000 | bytes 10000000 | tf_op jit(solution)/shard_map/first_step/pallas_call | solution.py:528
  73.5 1.8 %collective-permute-start.17 = (bf16[416,256]{1,0:T(8,128)(2,1)S(1)}, bf16[416,256]{1,0:T(8,128)(2,1)S(1)}, u32[]{:S(2)}, u32[]{:S(2)}) collective-permute-start(bf16[416,256]{1,0:T(8,128)(2,1)S(1)} %add_convert_fusion), channel_id=1, source_target_pairs={{0,6},{2,4},{4,2},{6,0},{1,7},{3,5},{5,3},{7,1},{8,14},{10,12},{12... | collective-permute-start | bytes 638984 | tf_op jit(solution)/shard_map/ppermute | solution.py:556
  75.6 2.4 %collective-permute-start.26 = (bf16[192,256]{1,0:T(8,128)(2,1)S(1)}, bf16[192,256]{1,0:T(8,128)(2,1)S(1)}, u32[]{:S(2)}, u32[]{:S(2)}) collective-permute-start(bf16[192,256]{1,0:T(8,128)(2,1)S(1)} %get-tuple-element.95), channel_id=1, source_target_pairs={{0,16},{8,24},{16,0},{24,8},{1,17},{9,25},{17,1},{25,9},{2,18},{10... | collective-permute-start | bytes 294920 | tf_op jit(solution)/shard_map/ppermute | solution.py:556
  78.2 2.0 %collective-permute-start.27 = (bf16[192,256]{1,0:T(8,128)(2,1)S(1)}, bf16[192,256]{1,0:T(8,128)(2,1)S(1)}, u32[]{:S(2)}, u32[]{:S(2)}) collective-permute-start(bf16[192,256]{1,0:T(8,128)(2,1)S(1)} %get-tuple-element.94), channel_id=1, source_target_pairs={{0,24},{8,16},{16,8},{24,0},{1,25},{9,17},{17,9},{25,1},{2,26},{10... | collective-permute-start | bytes 294920 | tf_op jit(solution)/shard_map/ppermute | solution.py:556
  80.3 3.0 %collective-permute-done.17 = bf16[416,256]{1,0:T(8,128)(2,1)S(1)} collective-permute-done((bf16[416,256]{1,0:T(8,128)(2,1)S(1)}, bf16[416,256]{1,0:T(8,128)(2,1)S(1)}, u32[]{:S(2)}, u32[]{:S(2)}) %collective-permute-start.17) | collective-permute-done | bytes 213024 | tf_op jit(solution)/shard_map/ppermute | solution.py:556
  83.5 2.5 %collective-permute-start.19 = (bf16[104,256]{1,0:T(8,128)(2,1)S(1)}, bf16[104,256]{1,0:T(8,128)(2,1)S(1)}, u32[]{:S(2)}, u32[]{:S(2)}) collective-permute-start(bf16[104,256]{1,0:T(8,128)(2,1)S(1)} %get-tuple-element.92), channel_id=1, source_target_pairs={{0,16},{8,24},{16,0},{24,8},{1,17},{9,25},{17,1},{25,9},{2,18},{10... | collective-permute-start | bytes 159752 | tf_op jit(solution)/shard_map/ppermute | solution.py:556
  87.1 2.0 %collective-permute-start.28 = (bf16[48,256]{1,0:T(8,128)(2,1)S(1)}, bf16[48,256]{1,0:T(8,128)(2,1)S(1)}, u32[]{:S(2)}, u32[]{:S(2)}) collective-permute-start(bf16[48,256]{1,0:T(8,128)(2,1)S(1)} %get-tuple-element.97), channel_id=1, source_target_pairs={{0,2},{2,0},{4,6},{6,4},{1,3},{3,1},{5,7},{7,5},{8,10},{10,8},{12,... | collective-permute-start | bytes 73736 | tf_op jit(solution)/shard_map/ppermute | solution.py:556
  91.2 1.7 %collective-permute-start.22 = (bf16[104,256]{1,0:T(8,128)(2,1)S(1)}, bf16[104,256]{1,0:T(8,128)(2,1)S(1)}, u32[]{:S(2)}, u32[]{:S(2)}) collective-permute-start(bf16[104,256]{1,0:T(8,128)(2,1)S(1)} %add_convert_fusion.8), channel_id=1, source_target_pairs={{0,16},{8,24},{16,0},{24,8},{1,17},{9,25},{17,1},{25,9},{2,18},{10... | collective-permute-start | bytes 159752 | tf_op jit(solution)/shard_map/ppermute | solution.py:556
  92.8 1.9 %collective-permute-start.23 = (bf16[104,256]{1,0:T(8,128)(2,1)S(1)}, bf16[104,256]{1,0:T(8,128)(2,1)S(1)}, u32[]{:S(2)}, u32[]{:S(2)}) collective-permute-start(bf16[104,256]{1,0:T(8,128)(2,1)S(1)} %add_convert_fusion.8), channel_id=1, source_target_pairs={{0,24},{8,16},{16,8},{24,0},{1,25},{9,17},{17,9},{25,1},{2,26},{10... | collective-permute-start | bytes 159752 | tf_op jit(solution)/shard_map/ppermute | solution.py:556
  94.7 1.9 %collective-permute-start.31 = (bf16[48,256]{1,0:T(8,128)(2,1)S(1)}, bf16[48,256]{1,0:T(8,128)(2,1)S(1)}, u32[]{:S(2)}, u32[]{:S(2)}) collective-permute-start(bf16[48,256]{1,0:T(8,128)(2,1)S(1)} %add_convert_fusion.13), channel_id=1, source_target_pairs={{0,2},{2,0},{4,6},{6,4},{1,3},{3,1},{5,7},{7,5},{8,10},{10,8},{12,... | collective-permute-start | bytes 73736 | tf_op jit(solution)/shard_map/ppermute | solution.py:556
  101.7 2.1 %collective-permute-start.43 = (bf16[192,256]{1,0:T(8,128)(2,1)S(1)}, bf16[192,256]{1,0:T(8,128)(2,1)S(1)}, u32[]{:S(2)}, u32[]{:S(2)}) collective-permute-start(bf16[192,256]{1,0:T(8,128)(2,1)S(1)} %pad_maximum_fusion.2), channel_id=1, source_target_pairs={{0,24},{8,16},{16,8},{24,0},{1,25},{9,17},{17,9},{25,1},{2,26},{10... | collective-permute-start | bytes 294920 | tf_op jit(solution)/shard_map/ppermute | solution.py:556
  107.1 6.8 %collective-permute-start.44 = (bf16[768,256]{1,0:T(8,128)(2,1)S(1)}, bf16[768,256]{1,0:T(8,128)(2,1)S(1)}, u32[]{:S(2)}, u32[]{:S(2)}) collective-permute-start(bf16[768,256]{1,0:T(8,128)(2,1)S(1)} %constant_dynamic-update-slice_fusion.refs_4_), channel_id=1, source_target_pairs={{0,1},{1,0},{2,3},{3,2},{4,5},{5,4},{6,7},{7,6},{8,9},{9,8},{10,11... | collective-permute-start | bytes 1179656 | tf_op jit(solution)/shard_map/ppermute | solution.py:556
  114.0 1.5 %collective-permute-start.36 = (bf16[416,256]{1,0:T(8,128)(2,1)S(1)}, bf16[416,256]{1,0:T(8,128)(2,1)S(1)}, u32[]{:S(2)}, u32[]{:S(2)}) collective-permute-start(bf16[416,256]{1,0:T(8,128)(2,1)S(1)} %collective-permute-done.35.refs_1_), channel_id=1, source_target_pairs={{0,1},{1,0},{2,3},{3,2},{4,5},{5,4},{6,7},{7,6},{8,9},{9,8},{10,11... | collective-permute-start | bytes 638984 | tf_op jit(solution)/shard_map/ppermute | solution.py:556
  115.5 2.4 %collective-permute-start.38 = (bf16[416,256]{1,0:T(8,128)(2,1)S(1)}, bf16[416,256]{1,0:T(8,128)(2,1)S(1)}, u32[]{:S(2)}, u32[]{:S(2)}) collective-permute-start(bf16[416,256]{1,0:T(8,128)(2,1)S(1)} %collective-permute-done.37.refs_2_), channel_id=1, source_target_pairs={{0,1},{1,0},{2,3},{3,2},{4,5},{5,4},{6,7},{7,6},{8,9},{9,8},{10,11... | collective-permute-start | bytes 638984 | tf_op jit(solution)/shard_map/ppermute | solution.py:556
  119.1 2.1 %assemble.2 = (f32[2304,256]{1,0:T(8,128)}, f32[2304,256]{1,0:T(8,128)}, f32[128,256]{1,0:T(8,128)S(1)}) custom-call(s32[6]{0:T(128)S(1)} %stack.35.place_ref.where_ref, bf16[416,256]{1,0:T(8,128)(2,1)S(1)} %pad_maximum_fusion.1.refs_0_, bf16[416,256]{1,0:T(8,128)(2,1)S(1)} %collective-permute-done.35.refs_1_, ...), custom_call_target="tpu_custom_call" | custom-call | flops 1000000 | bytes 3700000 | tf_op jit(solution)/shard_map/assemble/pallas_call | solution.py:625
  121.3 2.8 %assemble.3 = (f32[2304,256]{1,0:T(8,128)}, f32[2304,256]{1,0:T(8,128)}, f32[64,256]{1,0:T(8,128)}, f32[1,1]{1,0:T(1,128)}) custom-call(s32[6]{0:T(128)S(1)} %stack.35.place_ref.where_ref, bf16[416,256]{1,0:T(8,128)(2,1)S(1)} %collective-permute-done.34.refs_0_, ...), custom_call_target="tpu_custom_call", output_to_operand_aliasing={{0}: (6, {}), {1}: (7, {})} | custom-call | flops 1000000 | bytes 3700000 | tf_op jit(solution)/shard_map/assemble/pallas_call | solution.py:632
  (110 shorter events, 26.6 us)
Async XLA Ops:
  2.3 21.4 %collective-permute-start = (bf16[192,256]{1,0:T(8,128)(2,1)}, bf16[192,256]{1,0:T(8,128)(2,1)S(1)}, u32[]{:S(2)}, u32[]{:S(2)}) collective-permute-start(bf16[192,256]{1,0:T(8,128)(2,1)} %bitcast.6), channel_id=1, source_target_pairs={{0,1},{1,2},{2,3},{3,4},{4,5},{5,6},{6,7},{8,9},{9,10},{10,11},{11... | collective-permute-start | bytes 294920 | tf_op jit(solution)/shard_map/ppermute | solution.py:551
  6.8 16.9 %collective-permute-start.1 = (bf16[192,256]{1,0:T(8,128)(2,1)}, bf16[192,256]{1,0:T(8,128)(2,1)S(1)}, u32[]{:S(2)}, u32[]{:S(2)}) collective-permute-start(bf16[192,256]{1,0:T(8,128)(2,1)} %bitcast.7), channel_id=1, source_target_pairs={{1,0},{2,1},{3,2},{4,3},{5,4},{6,5},{7,6},{9,8},{10,9},{11,10},{12... | collective-permute-start | bytes 294920 | tf_op jit(solution)/shard_map/ppermute | solution.py:551
  14.0 23.6 %collective-permute-start.2 = (bf16[32,4224]{1,0:T(8,128)(2,1)}, bf16[32,4224]{1,0:T(8,128)(2,1)S(1)}, u32[]{:S(2)}, u32[]{:S(2)}) collective-permute-start(bf16[32,4224]{1,0:T(8,128)(2,1)} %get-tuple-element.53), channel_id=1, source_target_pairs={{0,24},{8,16},{16,8},{24,0},{1,25},{9,17},{17,9},{25,1},{2,26},{10... | collective-permute-start | bytes 811016 | tf_op jit(solution)/shard_map/ppermute | solution.py:556
  17.4 22.0 %collective-permute-start.3 = (bf16[32,4224]{1,0:T(8,128)(2,1)}, bf16[32,4224]{1,0:T(8,128)(2,1)S(1)}, u32[]{:S(2)}, u32[]{:S(2)}) collective-permute-start(bf16[32,4224]{1,0:T(8,128)(2,1)} %get-tuple-element.54), channel_id=1, source_target_pairs={{0,16},{8,24},{16,0},{24,8},{1,17},{9,25},{17,1},{25,9},{2,18},{10... | collective-permute-start | bytes 811016 | tf_op jit(solution)/shard_map/ppermute | solution.py:556
  23.0 16.5 %collective-permute-start.4 = (bf16[32,4224]{1,0:T(8,128)(2,1)}, bf16[32,4224]{1,0:T(8,128)(2,1)S(1)}, u32[]{:S(2)}, u32[]{:S(2)}) collective-permute-start(bf16[32,4224]{1,0:T(8,128)(2,1)} %get-tuple-element.55), channel_id=1, source_target_pairs={{0,8},{8,0},{16,24},{24,16},{1,9},{9,1},{17,25},{25,17},{2,10},{10... | collective-permute-start | bytes 811016 | tf_op jit(solution)/shard_map/ppermute | solution.py:556
  43.0 6.1 %collective-permute-start.7 = (bf16[16,4352]{1,0:T(8,128)(2,1)S(1)}, bf16[16,4352]{1,0:T(8,128)(2,1)S(1)}, u32[]{:S(2)}, u32[]{:S(2)}) collective-permute-start(bf16[16,4352]{1,0:T(8,128)(2,1)S(1)} %get-tuple-element.59), channel_id=1, source_target_pairs={{0,6},{2,4},{4,2},{6,0},{1,7},{3,5},{5,3},{7,1},{8,14},{10,12},{12... | collective-permute-start | bytes 417800 | tf_op jit(solution)/shard_map/ppermute | solution.py:556
  55.1 10.1 %collective-permute-start.10 = (bf16[128,256]{1,0:T(8,128)(2,1)S(1)}, bf16[128,256]{1,0:T(8,128)(2,1)S(1)}, u32[]{:S(2)}, u32[]{:S(2)}) collective-permute-start(bf16[128,256]{1,0:T(8,128)(2,1)S(1)} %get-tuple-element.61), channel_id=1, source_target_pairs={{1,0},{2,1},{3,2},{4,3},{5,4},{6,5},{7,6},{9,8},{10,9},{11,10},{12... | collective-permute-start | bytes 196616 | tf_op jit(solution)/shard_map/ppermute | solution.py:551
  57.4 7.8 %collective-permute-start.9 = (bf16[128,256]{1,0:T(8,128)(2,1)S(1)}, bf16[128,256]{1,0:T(8,128)(2,1)S(1)}, u32[]{:S(2)}, u32[]{:S(2)}) collective-permute-start(bf16[128,256]{1,0:T(8,128)(2,1)S(1)} %get-tuple-element.60), channel_id=1, source_target_pairs={{0,1},{1,2},{2,3},{3,4},{4,5},{5,6},{6,7},{8,9},{9,10},{10,11},{11... | collective-permute-start | bytes 196616 | tf_op jit(solution)/shard_map/ppermute | solution.py:551
  70.0 5.4 %collective-permute-start.24 = (bf16[768,256]{1,0:T(8,128)(2,1)S(1)}, bf16[768,256]{1,0:T(8,128)(2,1)S(1)}, u32[]{:S(2)}, u32[]{:S(2)}) collective-permute-start(bf16[768,256]{1,0:T(8,128)(2,1)S(1)} %get-tuple-element.78), channel_id=1, source_target_pairs={{0,1},{1,0},{2,3},{3,2},{4,5},{5,4},{6,7},{7,6},{8,9},{9,8},{10,11... | collective-permute-start | bytes 1179656 | tf_op jit(solution)/shard_map/ppermute | solution.py:556
  71.5 6.8 %collective-permute-start.13 = (bf16[416,256]{1,0:T(8,128)(2,1)S(1)}, bf16[416,256]{1,0:T(8,128)(2,1)S(1)}, u32[]{:S(2)}, u32[]{:S(2)}) collective-permute-start(bf16[416,256]{1,0:T(8,128)(2,1)S(1)} %add_convert_fusion.2), channel_id=1, source_target_pairs={{0,2},{2,0},{4,6},{6,4},{1,3},{3,1},{5,7},{7,5},{8,10},{10,8},{12,... | collective-permute-start | bytes 638984 | tf_op jit(solution)/shard_map/ppermute | solution.py:556
  72.9 7.4 %collective-permute-start.15 = (bf16[416,256]{1,0:T(8,128)(2,1)S(1)}, bf16[416,256]{1,0:T(8,128)(2,1)S(1)}, u32[]{:S(2)}, u32[]{:S(2)}) collective-permute-start(bf16[416,256]{1,0:T(8,128)(2,1)S(1)} %add_convert_fusion.1), channel_id=1, source_target_pairs={{0,4},{2,6},{4,0},{6,2},{1,5},{3,7},{5,1},{7,3},{8,12},{10,14},{12... | collective-permute-start | bytes 638984 | tf_op jit(solution)/shard_map/ppermute | solution.py:556
  73.5 9.8 %collective-permute-start.17 = (bf16[416,256]{1,0:T(8,128)(2,1)S(1)}, bf16[416,256]{1,0:T(8,128)(2,1)S(1)}, u32[]{:S(2)}, u32[]{:S(2)}) collective-permute-start(bf16[416,256]{1,0:T(8,128)(2,1)S(1)} %add_convert_fusion), channel_id=1, source_target_pairs={{0,6},{2,4},{4,2},{6,0},{1,7},{3,5},{5,3},{7,1},{8,14},{10,12},{12... | collective-permute-start | bytes 638984 | tf_op jit(solution)/shard_map/ppermute | solution.py:556
  75.5 10.4 %collective-permute-start.25 = (bf16[192,256]{1,0:T(8,128)(2,1)S(1)}, bf16[192,256]{1,0:T(8,128)(2,1)S(1)}, u32[]{:S(2)}, u32[]{:S(2)}) collective-permute-start(bf16[192,256]{1,0:T(8,128)(2,1)S(1)} %get-tuple-element.96), channel_id=1, source_target_pairs={{0,8},{8,0},{16,24},{24,16},{1,9},{9,1},{17,25},{25,17},{2,10},{10... | collective-permute-start | bytes 294920 | tf_op jit(solution)/shard_map/ppermute | solution.py:556
  75.6 11.4 %collective-permute-start.26 = (bf16[192,256]{1,0:T(8,128)(2,1)S(1)}, bf16[192,256]{1,0:T(8,128)(2,1)S(1)}, u32[]{:S(2)}, u32[]{:S(2)}) collective-permute-start(bf16[192,256]{1,0:T(8,128)(2,1)S(1)} %get-tuple-element.95), channel_id=1, source_target_pairs={{0,16},{8,24},{16,0},{24,8},{1,17},{9,25},{17,1},{25,9},{2,18},{10... | collective-permute-start | bytes 294920 | tf_op jit(solution)/shard_map/ppermute | solution.py:556
  78.2 8.8 %collective-permute-start.27 = (bf16[192,256]{1,0:T(8,128)(2,1)S(1)}, bf16[192,256]{1,0:T(8,128)(2,1)S(1)}, u32[]{:S(2)}, u32[]{:S(2)}) collective-permute-start(bf16[192,256]{1,0:T(8,128)(2,1)S(1)} %get-tuple-element.94), channel_id=1, source_target_pairs={{0,24},{8,16},{16,8},{24,0},{1,25},{9,17},{17,9},{25,1},{2,26},{10... | collective-permute-start | bytes 294920 | tf_op jit(solution)/shard_map/ppermute | solution.py:556
  83.4 5.7 %collective-permute-start.18 = (bf16[104,256]{1,0:T(8,128)(2,1)S(1)}, bf16[104,256]{1,0:T(8,128)(2,1)S(1)}, u32[]{:S(2)}, u32[]{:S(2)}) collective-permute-start(bf16[104,256]{1,0:T(8,128)(2,1)S(1)} %get-tuple-element.90), channel_id=1, source_target_pairs={{0,8},{8,0},{16,24},{24,16},{1,9},{9,1},{17,25},{25,17},{2,10},{10... | collective-permute-start | bytes 159752 | tf_op jit(solution)/shard_map/ppermute | solution.py:556
  83.5 6.8 %collective-permute-start.19 = (bf16[104,256]{1,0:T(8,128)(2,1)S(1)}, bf16[104,256]{1,0:T(8,128)(2,1)S(1)}, u32[]{:S(2)}, u32[]{:S(2)}) collective-permute-start(bf16[104,256]{1,0:T(8,128)(2,1)S(1)} %get-tuple-element.92), channel_id=1, source_target_pairs={{0,16},{8,24},{16,0},{24,8},{1,17},{9,25},{17,1},{25,9},{2,18},{10... | collective-permute-start | bytes 159752 | tf_op jit(solution)/shard_map/ppermute | solution.py:556
  87.1 5.7 %collective-permute-start.28 = (bf16[48,256]{1,0:T(8,128)(2,1)S(1)}, bf16[48,256]{1,0:T(8,128)(2,1)S(1)}, u32[]{:S(2)}, u32[]{:S(2)}) collective-permute-start(bf16[48,256]{1,0:T(8,128)(2,1)S(1)} %get-tuple-element.97), channel_id=1, source_target_pairs={{0,2},{2,0},{4,6},{6,4},{1,3},{3,1},{5,7},{7,5},{8,10},{10,8},{12,... | collective-permute-start | bytes 73736 | tf_op jit(solution)/shard_map/ppermute | solution.py:556
  89.1 5.6 %collective-permute-start.29 = (bf16[48,256]{1,0:T(8,128)(2,1)S(1)}, bf16[48,256]{1,0:T(8,128)(2,1)S(1)}, u32[]{:S(2)}, u32[]{:S(2)}) collective-permute-start(bf16[48,256]{1,0:T(8,128)(2,1)S(1)} %get-tuple-element.99), channel_id=1, source_target_pairs={{0,4},{2,6},{4,0},{6,2},{1,5},{3,7},{5,1},{7,3},{8,12},{10,14},{12... | collective-permute-start | bytes 73736 | tf_op jit(solution)/shard_map/ppermute | solution.py:556
  89.1 5.6 %collective-permute-start.30 = (bf16[48,256]{1,0:T(8,128)(2,1)S(1)}, bf16[48,256]{1,0:T(8,128)(2,1)S(1)}, u32[]{:S(2)}, u32[]{:S(2)}) collective-permute-start(bf16[48,256]{1,0:T(8,128)(2,1)S(1)} %get-tuple-element.98), channel_id=1, source_target_pairs={{0,6},{2,4},{4,2},{6,0},{1,7},{3,5},{5,3},{7,1},{8,14},{10,12},{12... | collective-permute-start | bytes 73736 | tf_op jit(solution)/shard_map/ppermute | solution.py:556
  91.1 5.6 %collective-permute-start.21 = (bf16[104,256]{1,0:T(8,128)(2,1)S(1)}, bf16[104,256]{1,0:T(8,128)(2,1)S(1)}, u32[]{:S(2)}, u32[]{:S(2)}) collective-permute-start(bf16[104,256]{1,0:T(8,128)(2,1)S(1)} %add_convert_fusion.8), channel_id=1, source_target_pairs={{0,8},{8,0},{16,24},{24,16},{1,9},{9,1},{17,25},{25,17},{2,10},{10... | collective-permute-start | bytes 159752 | tf_op jit(solution)/shard_map/ppermute | solution.py:556
  91.2 6.8 %collective-permute-start.22 = (bf16[104,256]{1,0:T(8,128)(2,1)S(1)}, bf16[104,256]{1,0:T(8,128)(2,1)S(1)}, u32[]{:S(2)}, u32[]{:S(2)}) collective-permute-start(bf16[104,256]{1,0:T(8,128)(2,1)S(1)} %add_convert_fusion.8), channel_id=1, source_target_pairs={{0,16},{8,24},{16,0},{24,8},{1,17},{9,25},{17,1},{25,9},{2,18},{10... | collective-permute-start | bytes 159752 | tf_op jit(solution)/shard_map/ppermute | solution.py:556
  100.3 5.4 %collective-permute-start.41 = (bf16[192,256]{1,0:T(8,128)(2,1)S(1)}, bf16[192,256]{1,0:T(8,128)(2,1)S(1)}, u32[]{:S(2)}, u32[]{:S(2)}) collective-permute-start(bf16[192,256]{1,0:T(8,128)(2,1)S(1)} %pad_maximum_fusion.2), channel_id=1, source_target_pairs={{0,8},{8,0},{16,24},{24,16},{1,9},{9,1},{17,25},{25,17},{2,10},{10... | collective-permute-start | bytes 294920 | tf_op jit(solution)/shard_map/ppermute | solution.py:556
  100.3 6.6 %collective-permute-start.42 = (bf16[192,256]{1,0:T(8,128)(2,1)S(1)}, bf16[192,256]{1,0:T(8,128)(2,1)S(1)}, u32[]{:S(2)}, u32[]{:S(2)}) collective-permute-start(bf16[192,256]{1,0:T(8,128)(2,1)S(1)} %pad_maximum_fusion.2), channel_id=1, source_target_pairs={{0,16},{8,24},{16,0},{24,8},{1,17},{9,25},{17,1},{25,9},{2,18},{10... | collective-permute-start | bytes 294920 | tf_op jit(solution)/shard_map/ppermute | solution.py:556
  101.7 5.3 %collective-permute-start.43 = (bf16[192,256]{1,0:T(8,128)(2,1)S(1)}, bf16[192,256]{1,0:T(8,128)(2,1)S(1)}, u32[]{:S(2)}, u32[]{:S(2)}) collective-permute-start(bf16[192,256]{1,0:T(8,128)(2,1)S(1)} %pad_maximum_fusion.2), channel_id=1, source_target_pairs={{0,24},{8,16},{16,8},{24,0},{1,25},{9,17},{17,9},{25,1},{2,26},{10... | collective-permute-start | bytes 294920 | tf_op jit(solution)/shard_map/ppermute | solution.py:556
  103.9 10.1 %collective-permute-start.35 = (bf16[416,256]{1,0:T(8,128)(2,1)S(1)}, bf16[416,256]{1,0:T(8,128)(2,1)S(1)}, u32[]{:S(2)}, u32[]{:S(2)}) collective-permute-start(bf16[416,256]{1,0:T(8,128)(2,1)S(1)} %pad_maximum_fusion.1.refs_0_), channel_id=1, source_target_pairs={{0,2},{2,0},{4,6},{6,4},{1,3},{3,1},{5,7},{7,5},{8,10},{10,8},{12,... | collective-permute-start | bytes 638984 | tf_op jit(solution)/shard_map/ppermute | solution.py:556
  104.8 10.7 %collective-permute-start.37 = (bf16[416,256]{1,0:T(8,128)(2,1)S(1)}, bf16[416,256]{1,0:T(8,128)(2,1)S(1)}, u32[]{:S(2)}, u32[]{:S(2)}) collective-permute-start(bf16[416,256]{1,0:T(8,128)(2,1)S(1)} %pad_maximum_fusion.1.refs_0_), channel_id=1, source_target_pairs={{0,4},{2,6},{4,0},{6,2},{1,5},{3,7},{5,1},{7,3},{8,12},{10,14},{12... | collective-permute-start | bytes 638984 | tf_op jit(solution)/shard_map/ppermute | solution.py:556
  105.7 12.2 %collective-permute-start.39 = (bf16[416,256]{1,0:T(8,128)(2,1)S(1)}, bf16[416,256]{1,0:T(8,128)(2,1)S(1)}, u32[]{:S(2)}, u32[]{:S(2)}) collective-permute-start(bf16[416,256]{1,0:T(8,128)(2,1)S(1)} %pad_maximum_fusion.1.refs_0_), channel_id=1, source_target_pairs={{0,6},{2,4},{4,2},{6,0},{1,7},{3,5},{5,3},{7,1},{8,14},{10,12},{12... | collective-permute-start | bytes 638984 | tf_op jit(solution)/shard_map/ppermute | solution.py:556
  107.1 14.2 %collective-permute-start.44 = (bf16[768,256]{1,0:T(8,128)(2,1)S(1)}, bf16[768,256]{1,0:T(8,128)(2,1)S(1)}, u32[]{:S(2)}, u32[]{:S(2)}) collective-permute-start(bf16[768,256]{1,0:T(8,128)(2,1)S(1)} %constant_dynamic-update-slice_fusion.refs_4_), channel_id=1, source_target_pairs={{0,1},{1,0},{2,3},{3,2},{4,5},{5,4},{6,7},{7,6},{8,9},{9,8},{10,11... | collective-permute-start | bytes 1179656 | tf_op jit(solution)/shard_map/ppermute | solution.py:556
  113.9 7.3 %collective-permute-start.34 = (bf16[416,256]{1,0:T(8,128)(2,1)S(1)}, bf16[416,256]{1,0:T(8,128)(2,1)S(1)}, u32[]{:S(2)}, u32[]{:S(2)}) collective-permute-start(bf16[416,256]{1,0:T(8,128)(2,1)S(1)} %pad_maximum_fusion.1.refs_0_), channel_id=1, source_target_pairs={{0,1},{1,0},{2,3},{3,2},{4,5},{5,4},{6,7},{7,6},{8,9},{9,8},{10,11... | collective-permute-start | bytes 638984 | tf_op jit(solution)/shard_map/ppermute | solution.py:556
  114.0 7.3 %collective-permute-start.36 = (bf16[416,256]{1,0:T(8,128)(2,1)S(1)}, bf16[416,256]{1,0:T(8,128)(2,1)S(1)}, u32[]{:S(2)}, u32[]{:S(2)}) collective-permute-start(bf16[416,256]{1,0:T(8,128)(2,1)S(1)} %collective-permute-done.35.refs_1_), channel_id=1, source_target_pairs={{0,1},{1,0},{2,3},{3,2},{4,5},{5,4},{6,7},{7,6},{8,9},{9,8},{10,11... | collective-permute-start | bytes 638984 | tf_op jit(solution)/shard_map/ppermute | solution.py:556
  115.5 5.7 %collective-permute-start.38 = (bf16[416,256]{1,0:T(8,128)(2,1)S(1)}, bf16[416,256]{1,0:T(8,128)(2,1)S(1)}, u32[]{:S(2)}, u32[]{:S(2)}) collective-permute-start(bf16[416,256]{1,0:T(8,128)(2,1)S(1)} %collective-permute-done.37.refs_2_), channel_id=1, source_target_pairs={{0,1},{1,0},{2,3},{3,2},{4,5},{5,4},{6,7},{7,6},{8,9},{9,8},{10,11... | collective-permute-start | bytes 638984 | tf_op jit(solution)/shard_map/ppermute | solution.py:556
  (21 other events, 89.6 us)

commit v2 on v0

--- a/solution.py
+++ b/solution.py
@@ -74,7 +74,7 @@
         pltpu.make_async_copy(logit_hbm.at[:, tile_rows, pl.ds(0, width)], x_ref.at[i], sems.at[i]).wait()
         each = range(parts)
         x = [x_ref[i, :, :, n * MXU : (n + 1) * MXU].astype(F32).reshape(members * tiles, MXU) for n in each]
-        root = [jnp.exp(one * 0.25) for one in x]
+        root = [jnp.exp2(one * (0.25 * math.log2(math.e))) for one in x]
         total = [dot(one.astype(BF16), same) for one in root]
         root = [one * pl.reciprocal(whole_sum, approx=True) for one, whole_sum in zip(root, total)]
         square = [one * one for one in root]

time: 125 us -> 124 us (level)
  no operation moved by 1% of the time
where the time goes in v2:
time: 124 us
  starting transfers between devices  63.6 us (51%)
  Pallas kernels  39.6 us (32%)
  waiting for transfers between devices  14.7 us (12%)
  local copies, waits for them, and re-layouts  4.32 us (3%)
  between operations  1.25 us (1%)
    ppermute x41, starting transfers between devices, pairwise(): return lax.ppermute(array, axis, [(i, i ^ step) for i in range(count)])  51.6 us
    ppermute x41, waiting for transfers between devices, pairwise(): return lax.ppermute(array, axis, [(i, i ^ step) for i in range(count)])  14.7 us
    ppermute x4, starting transfers between devices, neighbours(): return (lax.ppermute(last, axis, up), lax.ppermute(first, axis, down))  12 us
    pallas_call x2, Pallas kernels, teacher_moments(): pl.pallas_call(functools.partial(teacher_kernel, classes, flip), in_specs...  10.6 us
    pallas_call x1, Pallas kernels, student_forward(): pl.pallas_call(functools.partial(student_kernel, width), in_specs=[scalar...  9.12 us
    pallas_call x1, Pallas kernels, first_step(): pl.pallas_call(functools.partial(first_kernel, width, plan), in_specs=[sc...  4.65 us
    pallas_call x1, Pallas kernels, second_step(): pl.pallas_call(functools.partial(second_kernel, width), in_specs=whole(4)...  4.51 us
    pallas_call x1, Pallas kernels, assemble(): pl.pallas_call(kernel, in_specs=[scalars(), *whole(count), *hbm(2), *whol...  2.77 us
  transfers between devices with their start and end apart: 45, of which 13 were waited for; matrix products, arithmetic and copies ran while one was open for 1% of the time, Pallas kernels for 23%

profile of v2, /device:TPU:1, one launch (start us, length us, event | category | flops | bytes accessed | tf_op | source)
XLA Modules:
  0.0 124.1 jit_solution(14060352885418195549)
XLA Ops:
  0.6 1.6 %fusion = (bf16[1,3,64,256]{3,2,1,0:T(8,128)(2,1)}, bf16[1,3,64,256]{3,2,1,0:T(8,128)(2,1)}) fusion(bf16[1,32,64,256]{3,2,1,0:T(8,128)(2,1)} %param.9), kind=kLoop, calls=%fused_computation.26 | loop fusion | bytes 393216 | tf_op jit(solution)/shard_map/slice | solution.py:695
  2.3 4.5 %collective-permute-start = (bf16[192,256]{1,0:T(8,128)(2,1)}, bf16[192,256]{1,0:T(8,128)(2,1)S(1)}, u32[]{:S(2)}, u32[]{:S(2)}) collective-permute-start(bf16[192,256]{1,0:T(8,128)(2,1)} %bitcast.6), channel_id=1, source_target_pairs={{0,1},{1,2},{2,3},{3,4},{4,5},{5,6},{6,7},{8,9},{9,10},{10,11},{11... | collective-permute-start | bytes 294920 | tf_op jit(solution)/shard_map/ppermute | solution.py:545
  6.8 1.9 %collective-permute-start.1 = (bf16[192,256]{1,0:T(8,128)(2,1)}, bf16[192,256]{1,0:T(8,128)(2,1)S(1)}, u32[]{:S(2)}, u32[]{:S(2)}) collective-permute-start(bf16[192,256]{1,0:T(8,128)(2,1)} %bitcast.7), channel_id=1, source_target_pairs={{1,0},{2,1},{3,2},{4,3},{5,4},{6,5},{7,6},{9,8},{10,9},{11,10},{12... | collective-permute-start | bytes 294920 | tf_op jit(solution)/shard_map/ppermute | solution.py:545
  8.7 5.3 %teacher_moments.3 = (bf16[32,4224]{1,0:T(8,128)(2,1)}, bf16[32,4224]{1,0:T(8,128)(2,1)}) custom-call(bf16[4,128,4096]{2,1,0:T(8,128)(2,1)} %logit_hbm.3), custom_call_target="tpu_custom_call" | custom-call | flops 1500000000 | bytes 2600000 | tf_op jit(solution)/shard_map/teacher_moments/pallas_call | solution.py:111
  14.0 3.4 %collective-permute-start.2 = (bf16[32,4224]{1,0:T(8,128)(2,1)}, bf16[32,4224]{1,0:T(8,128)(2,1)S(1)}, u32[]{:S(2)}, u32[]{:S(2)}) collective-permute-start(bf16[32,4224]{1,0:T(8,128)(2,1)} %get-tuple-element.53), channel_id=1, source_target_pairs={{0,24},{8,16},{16,8},{24,0},{1,25},{9,17},{17,9},{25,1},{2,26},{10... | collective-permute-start | bytes 811016 | tf_op jit(solution)/shard_map/ppermute | solution.py:550
  17.5 5.4 %teacher_moments.2 = (bf16[32,4224]{1,0:T(8,128)(2,1)}, bf16[32,4224]{1,0:T(8,128)(2,1)}) custom-call(bf16[4,128,4096]{2,1,0:T(8,128)(2,1)} %logit_hbm.3), custom_call_target="tpu_custom_call" | custom-call | flops 1500000000 | bytes 2600000 | tf_op jit(solution)/shard_map/teacher_moments/pallas_call | solution.py:111
  25.8 9.1 %student_forward.1 = (bf16[2304,256]{1,0:T(8,128)(2,1)S(1)}, bf16[2048,256]{1,0:T(8,128)(2,1)S(1)}, f32[1024,128]{1,0:T(8,128)S(1)}, f32[1024,128]{1,0:T(8,128)S(1)}, f32[32,128]{1,0:T(8,128)S(1)}) custom-call(s32[6]{0:T(128)S(1)} %stack.35.place_ref.where_ref, bf16[192,256]{1,0:T(8,128)(2,1)S(1)} %collective-permute-done.before_ref, ...), custom_call_target="tpu_custom_call" | custom-call | flops 6000000000 | bytes 12000000 | tf_op jit(solution)/shard_map/student_forward/pallas_call | solution.py:278
  34.9 2.6 %turn.1 = (bf16[768,2176]{1,0:T(8,128)(2,1)S(1)}, bf16[768,2304]{1,0:T(8,128)(2,1)S(1)}, bf16[256,2048]{1,0:T(8,128)(2,1)S(1)}, bf16[3,768,256]{2,1,0:T(8,128)(2,1)S(1)}) custom-call(bf16[192,256]{1,0:T(8,128)(2,1)S(1)} %collective-permute-done.before_ref, bf16[2048,256]{1,0:T(8,128)(2,1)S(1)} %bitcast.23, ...), custom_call_target="tpu_custom_call" | custom-call | flops 3000000000 | bytes 14000000 | tf_op jit(solution)/shard_map/turn/pallas_call | solution.py:336
  37.5 1.9 %collective-permute-done.3.refs_1_ = bf16[32,4224]{1,0:T(8,128)(2,1)S(1)} collective-permute-done((bf16[32,4224]{1,0:T(8,128)(2,1)}, bf16[32,4224]{1,0:T(8,128)(2,1)S(1)}, u32[]{:S(2)}, u32[]{:S(2)}) %collective-permute-start.3) | collective-permute-done | bytes 270368 | tf_op jit(solution)/shard_map/ppermute | solution.py:550
  40.8 2.0 %collective-permute-start.5 = (bf16[16,4352]{1,0:T(8,128)(2,1)S(1)}, bf16[16,4352]{1,0:T(8,128)(2,1)S(1)}, u32[]{:S(2)}, u32[]{:S(2)}) collective-permute-start(bf16[16,4352]{1,0:T(8,128)(2,1)S(1)} %get-tuple-element.57), channel_id=1, source_target_pairs={{0,2},{2,0},{4,6},{6,4},{1,3},{3,1},{5,7},{7,5},{8,10},{10,8},{12,... | collective-permute-start | bytes 417800 | tf_op jit(solution)/shard_map/ppermute | solution.py:550
  45.3 2.2 %collective-permute-done.6.refs_2_ = bf16[16,4352]{1,0:T(8,128)(2,1)S(1)} collective-permute-done((bf16[16,4352]{1,0:T(8,128)(2,1)S(1)}, bf16[16,4352]{1,0:T(8,128)(2,1)S(1)}, u32[]{:S(2)}, u32[]{:S(2)}) %collective-permute-start.6) | collective-permute-done | bytes 139296 | tf_op jit(solution)/shard_map/ppermute | solution.py:550
  49.1 3.0 %collective-permute-start.8 = (bf16[32,4352]{1,0:T(8,128)(2,1)S(1)}, bf16[32,4352]{1,0:T(8,128)(2,1)S(1)}, u32[]{:S(2)}, u32[]{:S(2)}) collective-permute-start(bf16[32,4352]{1,0:T(8,128)(2,1)S(1)} %pad_maximum_fusion), channel_id=1, source_target_pairs={{0,1},{1,0},{2,3},{3,2},{4,5},{5,4},{6,7},{7,6},{8,9},{9,8},{10,11... | collective-permute-start | bytes 835592 | tf_op jit(solution)/shard_map/ppermute | solution.py:550
  53.3 1.8 %head_step.1 = (bf16[2048,256]{1,0:T(8,128)(2,1)S(1)}, bf16[128,256]{1,0:T(8,128)(2,1)S(1)}, bf16[128,256]{1,0:T(8,128)(2,1)S(1)}, f32[288,128]{1,0:T(8,128)S(1)}) custom-call(f32[1024,128]{1,0:T(8,128)S(1)} %get-tuple-element.47.log_ref, f32[1024,128]{1,0:T(8,128)S(1)} %get-tuple-element.48.base_ref, f32[32,128]{1,0:T(8,128)S(1)} %get-tuple-element.49.label_sum_ref, ...), custom_call_target="tpu_custom_call" | custom-call | flops 400000000 | bytes 5000000 | tf_op jit(solution)/shard_map/head_step/pallas_call | solution.py:404
  55.0 2.3 %collective-permute-start.10 = (bf16[128,256]{1,0:T(8,128)(2,1)S(1)}, bf16[128,256]{1,0:T(8,128)(2,1)S(1)}, u32[]{:S(2)}, u32[]{:S(2)}) collective-permute-start(bf16[128,256]{1,0:T(8,128)(2,1)S(1)} %get-tuple-element.61), channel_id=1, source_target_pairs={{1,0},{2,1},{3,2},{4,3},{5,4},{6,5},{7,6},{9,8},{10,9},{11,10},{12... | collective-permute-start | bytes 196616 | tf_op jit(solution)/shard_map/ppermute | solution.py:545
  57.3 3.3 %collective-permute-start.9 = (bf16[128,256]{1,0:T(8,128)(2,1)S(1)}, bf16[128,256]{1,0:T(8,128)(2,1)S(1)}, u32[]{:S(2)}, u32[]{:S(2)}) collective-permute-start(bf16[128,256]{1,0:T(8,128)(2,1)S(1)} %get-tuple-element.60), channel_id=1, source_target_pairs={{0,1},{1,2},{2,3},{3,4},{4,5},{5,6},{6,7},{8,9},{9,10},{10,11},{11... | collective-permute-start | bytes 196616 | tf_op jit(solution)/shard_map/ppermute | solution.py:545
  60.6 4.5 %second_step.1 = (bf16[2304,256]{1,0:T(8,128)(2,1)S(1)}, bf16[1536,256]{1,0:T(8,128)(2,1)S(1)}) custom-call(bf16[768,2304]{1,0:T(8,128)(2,1)S(1)} %get-tuple-element.64.ht_ref, bf16[2048,256]{1,0:T(8,128)(2,1)S(1)} %get-tuple-element.62.grad_ref, bf16[3,768,256]{2,1,0:T(8,128)(2,1)S(1)} %get-tuple-element.65.wt_ref.refs_0_, ...), custom_call_target="tpu_custom_call" | custom-call | flops 4499999744 | bytes 9000000 | tf_op jit(solution)/shard_map/second_step/pallas_call | solution.py:449
  65.2 4.7 %first_step.1 = (bf16[416,256]{1,0:T(8,128)(2,1)S(1)}, bf16[416,256]{1,0:T(8,128)(2,1)S(1)}, bf16[416,256]{1,0:T(8,128)(2,1)S(1)}, bf16[416,256]{1,0:T(8,128)(2,...) custom-call(s32[6]{0:T(128)S(1)} %stack.35.place_ref.where_ref, ...), custom_call_target="tpu_custom_call" | custom-call | flops 5000000000 | bytes 10000000 | tf_op jit(solution)/shard_map/first_step/pallas_call | solution.py:522
  73.5 1.8 %collective-permute-start.17 = (bf16[416,256]{1,0:T(8,128)(2,1)S(1)}, bf16[416,256]{1,0:T(8,128)(2,1)S(1)}, u32[]{:S(2)}, u32[]{:S(2)}) collective-permute-start(bf16[416,256]{1,0:T(8,128)(2,1)S(1)} %add_convert_fusion), channel_id=1, source_target_pairs={{0,6},{2,4},{4,2},{6,0},{1,7},{3,5},{5,3},{7,1},{8,14},{10,12},{12... | collective-permute-start | bytes 638984 | tf_op jit(solution)/shard_map/ppermute | solution.py:550
  75.5 2.4 %collective-permute-start.26 = (bf16[192,256]{1,0:T(8,128)(2,1)S(1)}, bf16[192,256]{1,0:T(8,128)(2,1)S(1)}, u32[]{:S(2)}, u32[]{:S(2)}) collective-permute-start(bf16[192,256]{1,0:T(8,128)(2,1)S(1)} %get-tuple-element.95), channel_id=1, source_target_pairs={{0,16},{8,24},{16,0},{24,8},{1,17},{9,25},{17,1},{25,9},{2,18},{10... | collective-permute-start | bytes 294920 | tf_op jit(solution)/shard_map/ppermute | solution.py:550
  78.2 2.0 %collective-permute-start.27 = (bf16[192,256]{1,0:T(8,128)(2,1)S(1)}, bf16[192,256]{1,0:T(8,128)(2,1)S(1)}, u32[]{:S(2)}, u32[]{:S(2)}) collective-permute-start(bf16[192,256]{1,0:T(8,128)(2,1)S(1)} %get-tuple-element.94), channel_id=1, source_target_pairs={{0,24},{8,16},{16,8},{24,0},{1,25},{9,17},{17,9},{25,1},{2,26},{10... | collective-permute-start | bytes 294920 | tf_op jit(solution)/shard_map/ppermute | solution.py:550
  80.2 3.0 %collective-permute-done.17 = bf16[416,256]{1,0:T(8,128)(2,1)S(1)} collective-permute-done((bf16[416,256]{1,0:T(8,128)(2,1)S(1)}, bf16[416,256]{1,0:T(8,128)(2,1)S(1)}, u32[]{:S(2)}, u32[]{:S(2)}) %collective-permute-start.17) | collective-permute-done | bytes 213024 | tf_op jit(solution)/shard_map/ppermute | solution.py:550
  83.4 2.4 %collective-permute-start.19 = (bf16[104,256]{1,0:T(8,128)(2,1)S(1)}, bf16[104,256]{1,0:T(8,128)(2,1)S(1)}, u32[]{:S(2)}, u32[]{:S(2)}) collective-permute-start(bf16[104,256]{1,0:T(8,128)(2,1)S(1)} %get-tuple-element.92), channel_id=1, source_target_pairs={{0,16},{8,24},{16,0},{24,8},{1,17},{9,25},{17,1},{25,9},{2,18},{10... | collective-permute-start | bytes 159752 | tf_op jit(solution)/shard_map/ppermute | solution.py:550
  87.0 2.0 %collective-permute-start.28 = (bf16[48,256]{1,0:T(8,128)(2,1)S(1)}, bf16[48,256]{1,0:T(8,128)(2,1)S(1)}, u32[]{:S(2)}, u32[]{:S(2)}) collective-permute-start(bf16[48,256]{1,0:T(8,128)(2,1)S(1)} %get-tuple-element.97), channel_id=1, source_target_pairs={{0,2},{2,0},{4,6},{6,4},{1,3},{3,1},{5,7},{7,5},{8,10},{10,8},{12,... | collective-permute-start | bytes 73736 | tf_op jit(solution)/shard_map/ppermute | solution.py:550
  91.1 1.7 %collective-permute-start.22 = (bf16[104,256]{1,0:T(8,128)(2,1)S(1)}, bf16[104,256]{1,0:T(8,128)(2,1)S(1)}, u32[]{:S(2)}, u32[]{:S(2)}) collective-permute-start(bf16[104,256]{1,0:T(8,128)(2,1)S(1)} %add_convert_fusion.8), channel_id=1, source_target_pairs={{0,16},{8,24},{16,0},{24,8},{1,17},{9,25},{17,1},{25,9},{2,18},{10... | collective-permute-start | bytes 159752 | tf_op jit(solution)/shard_map/ppermute | solution.py:550
  92.8 1.8 %collective-permute-start.23 = (bf16[104,256]{1,0:T(8,128)(2,1)S(1)}, bf16[104,256]{1,0:T(8,128)(2,1)S(1)}, u32[]{:S(2)}, u32[]{:S(2)}) collective-permute-start(bf16[104,256]{1,0:T(8,128)(2,1)S(1)} %add_convert_fusion.8), channel_id=1, source_target_pairs={{0,24},{8,16},{16,8},{24,0},{1,25},{9,17},{17,9},{25,1},{2,26},{10... | collective-permute-start | bytes 159752 | tf_op jit(solution)/shard_map/ppermute | solution.py:550
  94.6 2.0 %collective-permute-start.31 = (bf16[48,256]{1,0:T(8,128)(2,1)S(1)}, bf16[48,256]{1,0:T(8,128)(2,1)S(1)}, u32[]{:S(2)}, u32[]{:S(2)}) collective-permute-start(bf16[48,256]{1,0:T(8,128)(2,1)S(1)} %add_convert_fusion.13), channel_id=1, source_target_pairs={{0,2},{2,0},{4,6},{6,4},{1,3},{3,1},{5,7},{7,5},{8,10},{10,8},{12,... | collective-permute-start | bytes 73736 | tf_op jit(solution)/shard_map/ppermute | solution.py:550
  101.7 2.1 %collective-permute-start.43 = (bf16[192,256]{1,0:T(8,128)(2,1)S(1)}, bf16[192,256]{1,0:T(8,128)(2,1)S(1)}, u32[]{:S(2)}, u32[]{:S(2)}) collective-permute-start(bf16[192,256]{1,0:T(8,128)(2,1)S(1)} %pad_maximum_fusion.2), channel_id=1, source_target_pairs={{0,24},{8,16},{16,8},{24,0},{1,25},{9,17},{17,9},{25,1},{2,26},{10... | collective-permute-start | bytes 294920 | tf_op jit(solution)/shard_map/ppermute | solution.py:550
  107.0 6.8 %collective-permute-start.44 = (bf16[768,256]{1,0:T(8,128)(2,1)S(1)}, bf16[768,256]{1,0:T(8,128)(2,1)S(1)}, u32[]{:S(2)}, u32[]{:S(2)}) collective-permute-start(bf16[768,256]{1,0:T(8,128)(2,1)S(1)} %constant_dynamic-update-slice_fusion.refs_4_), channel_id=1, source_target_pairs={{0,1},{1,0},{2,3},{3,2},{4,5},{5,4},{6,7},{7,6},{8,9},{9,8},{10,11... | collective-permute-start | bytes 1179656 | tf_op jit(solution)/shard_map/ppermute | solution.py:550
  113.9 1.5 %collective-permute-start.36 = (bf16[416,256]{1,0:T(8,128)(2,1)S(1)}, bf16[416,256]{1,0:T(8,128)(2,1)S(1)}, u32[]{:S(2)}, u32[]{:S(2)}) collective-permute-start(bf16[416,256]{1,0:T(8,128)(2,1)S(1)} %collective-permute-done.35.refs_1_), channel_id=1, source_target_pairs={{0,1},{1,0},{2,3},{3,2},{4,5},{5,4},{6,7},{7,6},{8,9},{9,8},{10,11... | collective-permute-start | bytes 638984 | tf_op jit(solution)/shard_map/ppermute | solution.py:550
  115.4 2.4 %collective-permute-start.38 = (bf16[416,256]{1,0:T(8,128)(2,1)S(1)}, bf16[416,256]{1,0:T(8,128)(2,1)S(1)}, u32[]{:S(2)}, u32[]{:S(2)}) collective-permute-start(bf16[416,256]{1,0:T(8,128)(2,1)S(1)} %collective-permute-done.37.refs_2_), channel_id=1, source_target_pairs={{0,1},{1,0},{2,3},{3,2},{4,5},{5,4},{6,7},{7,6},{8,9},{9,8},{10,11... | collective-permute-start | bytes 638984 | tf_op jit(solution)/shard_map/ppermute | solution.py:550
  119.0 2.1 %assemble.2 = (f32[2304,256]{1,0:T(8,128)}, f32[2304,256]{1,0:T(8,128)}, f32[128,256]{1,0:T(8,128)S(1)}) custom-call(s32[6]{0:T(128)S(1)} %stack.35.place_ref.where_ref, bf16[416,256]{1,0:T(8,128)(2,1)S(1)} %pad_maximum_fusion.1.refs_0_, bf16[416,256]{1,0:T(8,128)(2,1)S(1)} %collective-permute-done.35.refs_1_, ...), custom_call_target="tpu_custom_call" | custom-call | flops 1000000 | bytes 3700000 | tf_op jit(solution)/shard_map/assemble/pallas_call | solution.py:619
  121.2 2.8 %assemble.3 = (f32[2304,256]{1,0:T(8,128)}, f32[2304,256]{1,0:T(8,128)}, f32[64,256]{1,0:T(8,128)}, f32[1,1]{1,0:T(1,128)}) custom-call(s32[6]{0:T(128)S(1)} %stack.35.place_ref.where_ref, bf16[416,256]{1,0:T(8,128)(2,1)S(1)} %collective-permute-done.34.refs_0_, ...), custom_call_target="tpu_custom_call", output_to_operand_aliasing={{0}: (6, {}), {1}: (7, {})} | custom-call | flops 1000000 | bytes 3700000 | tf_op jit(solution)/shard_map/assemble/pallas_call | solution.py:626
  (110 shorter events, 26.6 us)
Async XLA Ops:
  2.3 21.2 %collective-permute-start = (bf16[192,256]{1,0:T(8,128)(2,1)}, bf16[192,256]{1,0:T(8,128)(2,1)S(1)}, u32[]{:S(2)}, u32[]{:S(2)}) collective-permute-start(bf16[192,256]{1,0:T(8,128)(2,1)} %bitcast.6), channel_id=1, source_target_pairs={{0,1},{1,2},{2,3},{3,4},{4,5},{5,6},{6,7},{8,9},{9,10},{10,11},{11... | collective-permute-start | bytes 294920 | tf_op jit(solution)/shard_map/ppermute | solution.py:545
  6.8 16.7 %collective-permute-start.1 = (bf16[192,256]{1,0:T(8,128)(2,1)}, bf16[192,256]{1,0:T(8,128)(2,1)S(1)}, u32[]{:S(2)}, u32[]{:S(2)}) collective-permute-start(bf16[192,256]{1,0:T(8,128)(2,1)} %bitcast.7), channel_id=1, source_target_pairs={{1,0},{2,1},{3,2},{4,3},{5,4},{6,5},{7,6},{9,8},{10,9},{11,10},{12... | collective-permute-start | bytes 294920 | tf_op jit(solution)/shard_map/ppermute | solution.py:545
  14.0 23.6 %collective-permute-start.2 = (bf16[32,4224]{1,0:T(8,128)(2,1)}, bf16[32,4224]{1,0:T(8,128)(2,1)S(1)}, u32[]{:S(2)}, u32[]{:S(2)}) collective-permute-start(bf16[32,4224]{1,0:T(8,128)(2,1)} %get-tuple-element.53), channel_id=1, source_target_pairs={{0,24},{8,16},{16,8},{24,0},{1,25},{9,17},{17,9},{25,1},{2,26},{10... | collective-permute-start | bytes 811016 | tf_op jit(solution)/shard_map/ppermute | solution.py:550
  17.4 22.0 %collective-permute-start.3 = (bf16[32,4224]{1,0:T(8,128)(2,1)}, bf16[32,4224]{1,0:T(8,128)(2,1)S(1)}, u32[]{:S(2)}, u32[]{:S(2)}) collective-permute-start(bf16[32,4224]{1,0:T(8,128)(2,1)} %get-tuple-element.54), channel_id=1, source_target_pairs={{0,16},{8,24},{16,0},{24,8},{1,17},{9,25},{17,1},{25,9},{2,18},{10... | collective-permute-start | bytes 811016 | tf_op jit(solution)/shard_map/ppermute | solution.py:550
  22.8 16.6 %collective-permute-start.4 = (bf16[32,4224]{1,0:T(8,128)(2,1)}, bf16[32,4224]{1,0:T(8,128)(2,1)S(1)}, u32[]{:S(2)}, u32[]{:S(2)}) collective-permute-start(bf16[32,4224]{1,0:T(8,128)(2,1)} %get-tuple-element.55), channel_id=1, source_target_pairs={{0,8},{8,0},{16,24},{24,16},{1,9},{9,1},{17,25},{25,17},{2,10},{10... | collective-permute-start | bytes 811016 | tf_op jit(solution)/shard_map/ppermute | solution.py:550
  43.0 6.1 %collective-permute-start.7 = (bf16[16,4352]{1,0:T(8,128)(2,1)S(1)}, bf16[16,4352]{1,0:T(8,128)(2,1)S(1)}, u32[]{:S(2)}, u32[]{:S(2)}) collective-permute-start(bf16[16,4352]{1,0:T(8,128)(2,1)S(1)} %get-tuple-element.59), channel_id=1, source_target_pairs={{0,6},{2,4},{4,2},{6,0},{1,7},{3,5},{5,3},{7,1},{8,14},{10,12},{12... | collective-permute-start | bytes 417800 | tf_op jit(solution)/shard_map/ppermute | solution.py:550
  55.0 10.1 %collective-permute-start.10 = (bf16[128,256]{1,0:T(8,128)(2,1)S(1)}, bf16[128,256]{1,0:T(8,128)(2,1)S(1)}, u32[]{:S(2)}, u32[]{:S(2)}) collective-permute-start(bf16[128,256]{1,0:T(8,128)(2,1)S(1)} %get-tuple-element.61), channel_id=1, source_target_pairs={{1,0},{2,1},{3,2},{4,3},{5,4},{6,5},{7,6},{9,8},{10,9},{11,10},{12... | collective-permute-start | bytes 196616 | tf_op jit(solution)/shard_map/ppermute | solution.py:545
  57.3 7.8 %collective-permute-start.9 = (bf16[128,256]{1,0:T(8,128)(2,1)S(1)}, bf16[128,256]{1,0:T(8,128)(2,1)S(1)}, u32[]{:S(2)}, u32[]{:S(2)}) collective-permute-start(bf16[128,256]{1,0:T(8,128)(2,1)S(1)} %get-tuple-element.60), channel_id=1, source_target_pairs={{0,1},{1,2},{2,3},{3,4},{4,5},{5,6},{6,7},{8,9},{9,10},{10,11},{11... | collective-permute-start | bytes 196616 | tf_op jit(solution)/shard_map/ppermute | solution.py:545
  69.9 5.4 %collective-permute-start.24 = (bf16[768,256]{1,0:T(8,128)(2,1)S(1)}, bf16[768,256]{1,0:T(8,128)(2,1)S(1)}, u32[]{:S(2)}, u32[]{:S(2)}) collective-permute-start(bf16[768,256]{1,0:T(8,128)(2,1)S(1)} %get-tuple-element.78), channel_id=1, source_target_pairs={{0,1},{1,0},{2,3},{3,2},{4,5},{5,4},{6,7},{7,6},{8,9},{9,8},{10,11... | collective-permute-start | bytes 1179656 | tf_op jit(solution)/shard_map/ppermute | solution.py:550
  71.4 6.8 %collective-permute-start.13 = (bf16[416,256]{1,0:T(8,128)(2,1)S(1)}, bf16[416,256]{1,0:T(8,128)(2,1)S(1)}, u32[]{:S(2)}, u32[]{:S(2)}) collective-permute-start(bf16[416,256]{1,0:T(8,128)(2,1)S(1)} %add_convert_fusion.2), channel_id=1, source_target_pairs={{0,2},{2,0},{4,6},{6,4},{1,3},{3,1},{5,7},{7,5},{8,10},{10,8},{12,... | collective-permute-start | bytes 638984 | tf_op jit(solution)/shard_map/ppermute | solution.py:550
  72.8 7.4 %collective-permute-start.15 = (bf16[416,256]{1,0:T(8,128)(2,1)S(1)}, bf16[416,256]{1,0:T(8,128)(2,1)S(1)}, u32[]{:S(2)}, u32[]{:S(2)}) collective-permute-start(bf16[416,256]{1,0:T(8,128)(2,1)S(1)} %add_convert_fusion.1), channel_id=1, source_target_pairs={{0,4},{2,6},{4,0},{6,2},{1,5},{3,7},{5,1},{7,3},{8,12},{10,14},{12... | collective-permute-start | bytes 638984 | tf_op jit(solution)/shard_map/ppermute | solution.py:550
  73.5 9.8 %collective-permute-start.17 = (bf16[416,256]{1,0:T(8,128)(2,1)S(1)}, bf16[416,256]{1,0:T(8,128)(2,1)S(1)}, u32[]{:S(2)}, u32[]{:S(2)}) collective-permute-start(bf16[416,256]{1,0:T(8,128)(2,1)S(1)} %add_convert_fusion), channel_id=1, source_target_pairs={{0,6},{2,4},{4,2},{6,0},{1,7},{3,5},{5,3},{7,1},{8,14},{10,12},{12... | collective-permute-start | bytes 638984 | tf_op jit(solution)/shard_map/ppermute | solution.py:550
  75.4 10.4 %collective-permute-start.25 = (bf16[192,256]{1,0:T(8,128)(2,1)S(1)}, bf16[192,256]{1,0:T(8,128)(2,1)S(1)}, u32[]{:S(2)}, u32[]{:S(2)}) collective-permute-start(bf16[192,256]{1,0:T(8,128)(2,1)S(1)} %get-tuple-element.96), channel_id=1, source_target_pairs={{0,8},{8,0},{16,24},{24,16},{1,9},{9,1},{17,25},{25,17},{2,10},{10... | collective-permute-start | bytes 294920 | tf_op jit(solution)/shard_map/ppermute | solution.py:550
  75.5 11.4 %collective-permute-start.26 = (bf16[192,256]{1,0:T(8,128)(2,1)S(1)}, bf16[192,256]{1,0:T(8,128)(2,1)S(1)}, u32[]{:S(2)}, u32[]{:S(2)}) collective-permute-start(bf16[192,256]{1,0:T(8,128)(2,1)S(1)} %get-tuple-element.95), channel_id=1, source_target_pairs={{0,16},{8,24},{16,0},{24,8},{1,17},{9,25},{17,1},{25,9},{2,18},{10... | collective-permute-start | bytes 294920 | tf_op jit(solution)/shard_map/ppermute | solution.py:550
  78.2 8.8 %collective-permute-start.27 = (bf16[192,256]{1,0:T(8,128)(2,1)S(1)}, bf16[192,256]{1,0:T(8,128)(2,1)S(1)}, u32[]{:S(2)}, u32[]{:S(2)}) collective-permute-start(bf16[192,256]{1,0:T(8,128)(2,1)S(1)} %get-tuple-element.94), channel_id=1, source_target_pairs={{0,24},{8,16},{16,8},{24,0},{1,25},{9,17},{17,9},{25,1},{2,26},{10... | collective-permute-start | bytes 294920 | tf_op jit(solution)/shard_map/ppermute | solution.py:550
  83.3 5.7 %collective-permute-start.18 = (bf16[104,256]{1,0:T(8,128)(2,1)S(1)}, bf16[104,256]{1,0:T(8,128)(2,1)S(1)}, u32[]{:S(2)}, u32[]{:S(2)}) collective-permute-start(bf16[104,256]{1,0:T(8,128)(2,1)S(1)} %get-tuple-element.90), channel_id=1, source_target_pairs={{0,8},{8,0},{16,24},{24,16},{1,9},{9,1},{17,25},{25,17},{2,10},{10... | collective-permute-start | bytes 159752 | tf_op jit(solution)/shard_map/ppermute | solution.py:550
  83.4 6.8 %collective-permute-start.19 = (bf16[104,256]{1,0:T(8,128)(2,1)S(1)}, bf16[104,256]{1,0:T(8,128)(2,1)S(1)}, u32[]{:S(2)}, u32[]{:S(2)}) collective-permute-start(bf16[104,256]{1,0:T(8,128)(2,1)S(1)} %get-tuple-element.92), channel_id=1, source_target_pairs={{0,16},{8,24},{16,0},{24,8},{1,17},{9,25},{17,1},{25,9},{2,18},{10... | collective-permute-start | bytes 159752 | tf_op jit(solution)/shard_map/ppermute | solution.py:550
  87.0 5.7 %collective-permute-start.28 = (bf16[48,256]{1,0:T(8,128)(2,1)S(1)}, bf16[48,256]{1,0:T(8,128)(2,1)S(1)}, u32[]{:S(2)}, u32[]{:S(2)}) collective-permute-start(bf16[48,256]{1,0:T(8,128)(2,1)S(1)} %get-tuple-element.97), channel_id=1, source_target_pairs={{0,2},{2,0},{4,6},{6,4},{1,3},{3,1},{5,7},{7,5},{8,10},{10,8},{12,... | collective-permute-start | bytes 73736 | tf_op jit(solution)/shard_map/ppermute | solution.py:550
  89.0 5.6 %collective-permute-start.29 = (bf16[48,256]{1,0:T(8,128)(2,1)S(1)}, bf16[48,256]{1,0:T(8,128)(2,1)S(1)}, u32[]{:S(2)}, u32[]{:S(2)}) collective-permute-start(bf16[48,256]{1,0:T(8,128)(2,1)S(1)} %get-tuple-element.99), channel_id=1, source_target_pairs={{0,4},{2,6},{4,0},{6,2},{1,5},{3,7},{5,1},{7,3},{8,12},{10,14},{12... | collective-permute-start | bytes 73736 | tf_op jit(solution)/shard_map/ppermute | solution.py:550
  89.0 5.6 %collective-permute-start.30 = (bf16[48,256]{1,0:T(8,128)(2,1)S(1)}, bf16[48,256]{1,0:T(8,128)(2,1)S(1)}, u32[]{:S(2)}, u32[]{:S(2)}) collective-permute-start(bf16[48,256]{1,0:T(8,128)(2,1)S(1)} %get-tuple-element.98), channel_id=1, source_target_pairs={{0,6},{2,4},{4,2},{6,0},{1,7},{3,5},{5,3},{7,1},{8,14},{10,12},{12... | collective-permute-start | bytes 73736 | tf_op jit(solution)/shard_map/ppermute | solution.py:550
  91.0 5.6 %collective-permute-start.21 = (bf16[104,256]{1,0:T(8,128)(2,1)S(1)}, bf16[104,256]{1,0:T(8,128)(2,1)S(1)}, u32[]{:S(2)}, u32[]{:S(2)}) collective-permute-start(bf16[104,256]{1,0:T(8,128)(2,1)S(1)} %add_convert_fusion.8), channel_id=1, source_target_pairs={{0,8},{8,0},{16,24},{24,16},{1,9},{9,1},{17,25},{25,17},{2,10},{10... | collective-permute-start | bytes 159752 | tf_op jit(solution)/shard_map/ppermute | solution.py:550
  91.1 6.8 %collective-permute-start.22 = (bf16[104,256]{1,0:T(8,128)(2,1)S(1)}, bf16[104,256]{1,0:T(8,128)(2,1)S(1)}, u32[]{:S(2)}, u32[]{:S(2)}) collective-permute-start(bf16[104,256]{1,0:T(8,128)(2,1)S(1)} %add_convert_fusion.8), channel_id=1, source_target_pairs={{0,16},{8,24},{16,0},{24,8},{1,17},{9,25},{17,1},{25,9},{2,18},{10... | collective-permute-start | bytes 159752 | tf_op jit(solution)/shard_map/ppermute | solution.py:550
  100.2 5.4 %collective-permute-start.41 = (bf16[192,256]{1,0:T(8,128)(2,1)S(1)}, bf16[192,256]{1,0:T(8,128)(2,1)S(1)}, u32[]{:S(2)}, u32[]{:S(2)}) collective-permute-start(bf16[192,256]{1,0:T(8,128)(2,1)S(1)} %pad_maximum_fusion.2), channel_id=1, source_target_pairs={{0,8},{8,0},{16,24},{24,16},{1,9},{9,1},{17,25},{25,17},{2,10},{10... | collective-permute-start | bytes 294920 | tf_op jit(solution)/shard_map/ppermute | solution.py:550
  100.3 6.6 %collective-permute-start.42 = (bf16[192,256]{1,0:T(8,128)(2,1)S(1)}, bf16[192,256]{1,0:T(8,128)(2,1)S(1)}, u32[]{:S(2)}, u32[]{:S(2)}) collective-permute-start(bf16[192,256]{1,0:T(8,128)(2,1)S(1)} %pad_maximum_fusion.2), channel_id=1, source_target_pairs={{0,16},{8,24},{16,0},{24,8},{1,17},{9,25},{17,1},{25,9},{2,18},{10... | collective-permute-start | bytes 294920 | tf_op jit(solution)/shard_map/ppermute | solution.py:550
  101.7 5.3 %collective-permute-start.43 = (bf16[192,256]{1,0:T(8,128)(2,1)S(1)}, bf16[192,256]{1,0:T(8,128)(2,1)S(1)}, u32[]{:S(2)}, u32[]{:S(2)}) collective-permute-start(bf16[192,256]{1,0:T(8,128)(2,1)S(1)} %pad_maximum_fusion.2), channel_id=1, source_target_pairs={{0,24},{8,16},{16,8},{24,0},{1,25},{9,17},{17,9},{25,1},{2,26},{10... | collective-permute-start | bytes 294920 | tf_op jit(solution)/shard_map/ppermute | solution.py:550
  103.8 10.1 %collective-permute-start.35 = (bf16[416,256]{1,0:T(8,128)(2,1)S(1)}, bf16[416,256]{1,0:T(8,128)(2,1)S(1)}, u32[]{:S(2)}, u32[]{:S(2)}) collective-permute-start(bf16[416,256]{1,0:T(8,128)(2,1)S(1)} %pad_maximum_fusion.1.refs_0_), channel_id=1, source_target_pairs={{0,2},{2,0},{4,6},{6,4},{1,3},{3,1},{5,7},{7,5},{8,10},{10,8},{12,... | collective-permute-start | bytes 638984 | tf_op jit(solution)/shard_map/ppermute | solution.py:550
  104.7 10.7 %collective-permute-start.37 = (bf16[416,256]{1,0:T(8,128)(2,1)S(1)}, bf16[416,256]{1,0:T(8,128)(2,1)S(1)}, u32[]{:S(2)}, u32[]{:S(2)}) collective-permute-start(bf16[416,256]{1,0:T(8,128)(2,1)S(1)} %pad_maximum_fusion.1.refs_0_), channel_id=1, source_target_pairs={{0,4},{2,6},{4,0},{6,2},{1,5},{3,7},{5,1},{7,3},{8,12},{10,14},{12... | collective-permute-start | bytes 638984 | tf_op jit(solution)/shard_map/ppermute | solution.py:550
  105.6 12.2 %collective-permute-start.39 = (bf16[416,256]{1,0:T(8,128)(2,1)S(1)}, bf16[416,256]{1,0:T(8,128)(2,1)S(1)}, u32[]{:S(2)}, u32[]{:S(2)}) collective-permute-start(bf16[416,256]{1,0:T(8,128)(2,1)S(1)} %pad_maximum_fusion.1.refs_0_), channel_id=1, source_target_pairs={{0,6},{2,4},{4,2},{6,0},{1,7},{3,5},{5,3},{7,1},{8,14},{10,12},{12... | collective-permute-start | bytes 638984 | tf_op jit(solution)/shard_map/ppermute | solution.py:550
  107.0 14.2 %collective-permute-start.44 = (bf16[768,256]{1,0:T(8,128)(2,1)S(1)}, bf16[768,256]{1,0:T(8,128)(2,1)S(1)}, u32[]{:S(2)}, u32[]{:S(2)}) collective-permute-start(bf16[768,256]{1,0:T(8,128)(2,1)S(1)} %constant_dynamic-update-slice_fusion.refs_4_), channel_id=1, source_target_pairs={{0,1},{1,0},{2,3},{3,2},{4,5},{5,4},{6,7},{7,6},{8,9},{9,8},{10,11... | collective-permute-start | bytes 1179656 | tf_op jit(solution)/shard_map/ppermute | solution.py:550
  113.8 7.3 %collective-permute-start.34 = (bf16[416,256]{1,0:T(8,128)(2,1)S(1)}, bf16[416,256]{1,0:T(8,128)(2,1)S(1)}, u32[]{:S(2)}, u32[]{:S(2)}) collective-permute-start(bf16[416,256]{1,0:T(8,128)(2,1)S(1)} %pad_maximum_fusion.1.refs_0_), channel_id=1, source_target_pairs={{0,1},{1,0},{2,3},{3,2},{4,5},{5,4},{6,7},{7,6},{8,9},{9,8},{10,11... | collective-permute-start | bytes 638984 | tf_op jit(solution)/shard_map/ppermute | solution.py:550
  113.9 7.3 %collective-permute-start.36 = (bf16[416,256]{1,0:T(8,128)(2,1)S(1)}, bf16[416,256]{1,0:T(8,128)(2,1)S(1)}, u32[]{:S(2)}, u32[]{:S(2)}) collective-permute-start(bf16[416,256]{1,0:T(8,128)(2,1)S(1)} %collective-permute-done.35.refs_1_), channel_id=1, source_target_pairs={{0,1},{1,0},{2,3},{3,2},{4,5},{5,4},{6,7},{7,6},{8,9},{9,8},{10,11... | collective-permute-start | bytes 638984 | tf_op jit(solution)/shard_map/ppermute | solution.py:550
  115.4 5.7 %collective-permute-start.38 = (bf16[416,256]{1,0:T(8,128)(2,1)S(1)}, bf16[416,256]{1,0:T(8,128)(2,1)S(1)}, u32[]{:S(2)}, u32[]{:S(2)}) collective-permute-start(bf16[416,256]{1,0:T(8,128)(2,1)S(1)} %collective-permute-done.37.refs_2_), channel_id=1, source_target_pairs={{0,1},{1,0},{2,3},{3,2},{4,5},{5,4},{6,7},{7,6},{8,9},{9,8},{10,11... | collective-permute-start | bytes 638984 | tf_op jit(solution)/shard_map/ppermute | solution.py:550
  (21 other events, 89.2 us)
